TPU v7x, 32 devices: a whole 2x2x4 slice. The times are simulated.
32 devices in a mesh: seq: 8 (over z, y), head: 4 (over x, core).
Axes of the slice: x: 2, y: 2, z: 4, core: 2. Of those that a mesh axis runs over, the one named last changes fastest.
Arguments:
- tokens: bfloat16 [65536, 512], P(('seq', 'head')), may hold values from -6 to 6
- gain_first: float32 [512], replicated, may hold values from 0.5 to 1.5
- w_query: bfloat16 [512, 512], P(None, 'head'), may hold values from -0.5 to 0.5
- w_key: bfloat16 [512, 512], P(None, 'head'), may hold values from -0.25 to 0.25
- w_value: bfloat16 [512, 512], P(None, 'head'), may hold values from -0.25 to 0.25
- w_out: bfloat16 [512, 512], P('head'), may hold values from -1 to 1
- gain_second: float32 [512], replicated, may hold values from 0.5 to 1.5
- w_control: bfloat16 [512, 8], replicated, may hold values from -0.125 to 0.125
- w_expand: bfloat16 [8, 512, 2048], P('seq'), may hold values from -1.5 to 1.5
- b_expand: float32 [8, 2048], P('seq'), may hold values from -1 to 1
- w_reduce: bfloat16 [8, 2048, 512], P('seq'), may hold values from -1 to 1
- b_reduce: float32 [8, 512], P('seq'), may hold values from -3 to 3
- lengths: int32 [8, 32], P('seq'), may hold values from 0 to 1024, as said below
- grad_output: bfloat16 [65536, 512], P(('seq', 'head')), may hold values from -6 to 6
Outputs:
- output: bfloat16 [65536, 512], P(('seq', 'head'))
- grad_tokens: float32 [65536, 512], P(('seq', 'head'))
- grad_gain_first: float32 [512], replicated
- grad_query: float32 [512, 512], P(None, 'head')
- grad_key: float32 [512, 512], P(None, 'head')
- grad_value: float32 [512, 512], P(None, 'head')
- grad_w_out: float32 [512, 512], P('head')
- grad_gain_second: float32 [512], replicated
- grad_control: float32 [512, 8], replicated
- grad_expand: float32 [8, 512, 2048], P('seq')
- grad_expand_bias: float32 [8, 2048], P('seq')
- grad_reduce: float32 [8, 2048, 512], P('seq')
- grad_reduce_bias: float32 [8, 512], P('seq')
Inputs may be any that keep to these rules, and one draw needn't show every extreme that they name: Row s lists, in order, the lengths of the sequences packed in the 8192 places of index s of seq, 8 blocks of four entries, one block for each 1024 places; a block is either one sequence of 1024 tokens followed by three zeros or four sequences of 64 to 448 tokens that sum to 1024. A row is of one kind throughout, and both kinds occur in every draw.
All inputs are finite; a program needn't handle non-finite values.
Results may differ from a plain program's by a relative error of at most 0.028.
Values may be sent and summed in bfloat16 or wider, within the bound.
No kernel may reach another device: no remote copies, remote signals or barrier semaphores. Data moves between devices by JAX's collectives and lax.ppermute only.
A program may use at most 192 MiB of HBM per device.

v0:
```python
import functools
import jax
import jax.numpy as jnp
from jax import lax
from jax.sharding import PartitionSpec as P
from jax.experimental import pallas as pl
from jax.experimental.pallas import tpu as pltpu

HEAD_DIM = 64
GROUP = 32
LONG = 1024
TILE = 256
QUEUE = 32
EPSILON = 1e-05
MASKED = -1000000000.0
BF = jnp.bfloat16
F32 = jnp.float32
ROWS_BY_ROWS = (((0,), (0,)), ((), ()))
COLS_BY_COLS = (((1,), (1,)), ((), ()))
VMEM_LIMIT = 62 * 1024 * 1024


def dot(left, right):
    return jnp.dot(left, right, preferred_element_type=F32)


def dot_rows(left, right):
    return lax.dot_general(left, right, ROWS_BY_ROWS, preferred_element_type=F32)


def dot_cols(left, right):
    return lax.dot_general(left, right, COLS_BY_COLS, preferred_element_type=F32)


def normalize(matrix):
    centre = jnp.mean(matrix, axis=1, keepdims=True)
    shifted = matrix - centre
    scaling = lax.rsqrt(jnp.mean(shifted * shifted, axis=1, keepdims=True) + EPSILON)
    return shifted * scaling, scaling


def normalize_back(grad_norm, gain, unit_rows, scaling):
    inner_grad = grad_norm * gain
    centred = (
        inner_grad
        - jnp.mean(inner_grad, axis=1, keepdims=True)
        - unit_rows * jnp.mean(inner_grad * unit_rows, axis=1, keepdims=True)
    )
    return scaling * centred, jnp.sum(grad_norm * unit_rows, axis=0, keepdims=True)


def whole(*shape):
    return pl.BlockSpec(shape, lambda *_: (0,) * len(shape))


def scalars():
    return pl.BlockSpec(memory_space=pltpu.SMEM)


def call(kernel, name, grid, in_specs, out_specs, out_shape, scratch=(), cost=(0, 0, 0), aliases=None):
    return pl.pallas_call(
        kernel,
        grid=grid,
        in_specs=in_specs,
        out_specs=out_specs,
        out_shape=out_shape,
        scratch_shapes=list(scratch),
        input_output_aliases=aliases or {},
        cost_estimate=pl.CostEstimate(
            flops=int(cost[0]), bytes_accessed=int(cost[1]), transcendentals=int(cost[2])
        ),
        compiler_params=pltpu.CompilerParams(vmem_limit_bytes=VMEM_LIMIT),
        name=name,
    )


def shape(dims, dtype):
    return jax.ShapeDtypeStruct(dims, dtype)


def tile_slot(row_tile, col_tile):
    return row_tile * (row_tile + 1) // 2 + col_tile


def halves(dtype):
    lane = lax.broadcasted_iota(jnp.int32, (1, 2 * HEAD_DIM), 1)
    first = (lane < HEAD_DIM).astype(F32)
    return first.astype(dtype), (1.0 - first).astype(dtype)


def load_weights(step, order, parts, w_now, o_now):
    width = w_now.shape[0] if w_now is not None else o_now.shape[1]
    for index, part in enumerate(parts):

        @pl.when(step == order(index))
        def _(part=part):
            cut = part.shape[1]
            if w_now is not None:
                for block in range(3):
                    w_now[:, block * cut : (block + 1) * cut] = part[block * width : (block + 1) * width]
            if o_now is not None:
                for block in range(width // cut):
                    begin = 3 * width + block * cut
                    o_now[:, block * cut : (block + 1) * cut] = part[begin : begin + cut]


def forward_kernel(pairs, chunk, chunks, *refs):
    place, lengths, tokens, gain_first = refs[:4]
    parts = refs[4 : 4 + pairs]
    gain_second = refs[4 + pairs]
    normed, qkv_out, exps, inverse, attended, resid, second = refs[5 + pairs : 12 + pairs]
    w_now, bias, attended_all = refs[12 + pairs :]
    step = pl.program_id(0)
    width = tokens.shape[1]
    pair_width = attended.shape[2]
    tiles = LONG // TILE

    @pl.when(step == 0)
    def _():
        unit, _ = normalize(tokens[...].astype(F32))
        normed[...] = (unit * gain_first[...]).astype(BF)
        base = 4 * (place[1] * chunks + chunk)
        first = lengths[0, base]
        second_bound = first + lengths[0, base + 1]
        third = second_bound + lengths[0, base + 2]
        for row_tile in range(tiles):
            row = lax.broadcasted_iota(jnp.int32, (TILE, 1), 0) + row_tile * TILE
            begin = jnp.where(row >= first, first, 0)
            begin = jnp.where(row >= second_bound, second_bound, begin)
            begin = jnp.where(row >= third, third, begin)
            col = lax.broadcasted_iota(jnp.int32, (TILE, LONG), 1)
            allowed = (col <= row) & (col >= begin)
            bias[pl.ds(row_tile * TILE, TILE), :] = jnp.where(allowed, 0.0, MASKED)

    load_weights(step, lambda index: index, parts, w_now, None)
    qkv = dot(normed[...], w_now[...]).astype(BF)
    qkv_out[0] = qkv
    queries = qkv[:, :pair_width] * BF(HEAD_DIM**-0.5)
    key_rows = qkv[:, pair_width : 2 * pair_width]
    value_rows = qkv[:, 2 * pair_width :]
    low_half, high_half = halves(BF)
    is_low = lax.broadcasted_iota(jnp.int32, (TILE, pair_width), 1) < HEAD_DIM
    masks = ((low_half, high_half), (high_half, low_half))
    head_queries = [queries * own for own, other in masks]
    head_values = [value_rows * own + other for own, other in masks]
    for row_tile in range(tiles):
        begin, extent = row_tile * TILE, (row_tile + 1) * TILE
        raw = []
        for head in range(2):
            scores = dot_cols(head_queries[head][begin:extent], key_rows[:extent])
            scores = scores + bias[begin:extent, :extent]
            highest = jnp.max(scores, axis=1, keepdims=True)
            powers = jnp.exp(scores - highest).astype(BF)
            for col_tile in range(row_tile + 1):
                exps[0, head, tile_slot(row_tile, col_tile)] = powers[
                    :, col_tile * TILE : (col_tile + 1) * TILE
                ]
            raw.append(dot(powers, head_values[head][:extent]))
        totals = jnp.where(
            is_low, pltpu.roll(raw[0], HEAD_DIM, 1), pltpu.roll(raw[1], HEAD_DIM, 1)
        )
        inverted = 1.0 / totals
        inverse[0, begin:extent] = inverted
        attended_tile = (jnp.where(is_low, raw[0], raw[1]) * inverted).astype(BF)
        attended[0, begin:extent] = attended_tile
        attended_all[step, begin:extent] = attended_tile

    @pl.when(step == pairs - 1)
    def _():
        rows = jnp.concatenate([attended_all[index] for index in range(pairs)], axis=1)
        blocks = width // pair_width
        weights = jnp.concatenate(
            [
                jnp.concatenate(
                    [
                        part[3 * width + block * pair_width : 3 * width + (block + 1) * pair_width]
                        for block in range(blocks)
                    ],
                    axis=1,
                )
                for part in parts
            ],
            axis=0,
        )
        total = tokens[...].astype(F32) + dot(rows, weights)
        resid[...] = total
        unit, _ = normalize(total)
        second[...] = (unit * gain_second[...]).astype(BF)


def forward_part(chunk, place, lengths, tokens, gain_first, parts, gain_second):
    rows, width = tokens.shape
    pairs = len(parts)
    packed, pair_width = parts[0].shape
    triple = 3 * pair_width
    kept = LONG // TILE * (LONG // TILE + 1) // 2
    per_pair = lambda *dims: pl.BlockSpec((1,) + dims, lambda i: (i,) + (0,) * len(dims))
    return call(
        functools.partial(forward_kernel, pairs, chunk, rows // LONG),
        f"forward_{chunk}",
        (pairs,),
        [scalars(), scalars(), pl.BlockSpec((LONG, width), lambda i: (chunk, 0)), whole(1, width)]
        + [whole(packed, pair_width)] * pairs
        + [whole(1, width)],
        [
            whole(LONG, width),
            per_pair(LONG, triple),
            per_pair(2, kept, TILE, TILE),
            per_pair(LONG, pair_width),
            per_pair(LONG, pair_width),
            whole(LONG, width),
            whole(LONG, width),
        ],
        [
            shape((LONG, width), BF),
            shape((pairs, LONG, triple), BF),
            shape((pairs, 2, kept, TILE, TILE), BF),
            shape((pairs, LONG, pair_width), F32),
            shape((pairs, LONG, pair_width), BF),
            shape((LONG, width), F32),
            shape((LONG, width), BF),
        ],
        [
            pltpu.VMEM((width, triple), BF),
            pltpu.VMEM((LONG, LONG), F32),
            pltpu.VMEM((pairs, LONG, pair_width), BF),
        ],
        (10e9, 25e6, 5e6),
    )(place, lengths, tokens, gain_first, *parts, gain_second)


def pack_kernel(slots, chunks, rows, out):
    share = LONG // slots
    for chunk in range(chunks):
        for index in range(slots):
            begin = chunk * LONG + index * share
            out[index, chunk] = rows[begin : begin + share, :]


def pack_rows(rows, slots):
    total, width = rows.shape
    chunks, share = total // LONG, LONG // slots
    return call(
        functools.partial(pack_kernel, slots, chunks),
        "pack_cotangent",
        (1,),
        [whole(total, width)],
        whole(slots, chunks, share, width),
        shape((slots, chunks, share, width), BF),
        cost=(0, 4 * total * width, 0),
    )(rows)


def pack_weights_kernel(query, key, value, out, packed):
    width, cut = query.shape
    for index, part in enumerate((query, key, value)):
        packed[index * width : (index + 1) * width] = part[...]
    for index in range(width // cut):
        begin = 3 * width + index * cut
        packed[begin : begin + cut] = out[:, index * cut : (index + 1) * cut]


def pack_weights(query, key, value, out):
    width, cut = query.shape
    return call(
        pack_weights_kernel,
        "pack_weights",
        (1,),
        [whole(width, cut)] * 3 + [whole(cut, width)],
        whole(4 * width, cut),
        shape((4 * width, cut), BF),
        cost=(0, 16 * width * cut, 0),
    )(query, key, value, out)


def group_mask(slots, columns):
    share = LONG // slots
    stride = share // QUEUE
    row = lax.broadcasted_iota(jnp.int32, (LONG, columns), 0)
    col = lax.broadcasted_iota(jnp.int32, (LONG, columns), 1)
    return ((row % share) // stride) == (col % QUEUE)


def mixing_kernel(slots, control, members, cotangents, mixing_out, messages):
    width, columns = control.shape
    rows = members[...]
    grads = cotangents[...].reshape(LONG, width)
    logits = jnp.where(group_mask(slots, columns), dot(rows, control[...]), -1e30)
    powers = jnp.exp(logits - jnp.max(logits, axis=0, keepdims=True))
    mixing = powers / jnp.sum(powers, axis=0, keepdims=True)
    mixing_out[...] = mixing
    low = mixing.astype(BF)
    mixed = dot_rows(low, rows).astype(BF)
    grad_out = dot_rows(low, grads).astype(BF)
    for index in range(slots):
        part = slice(index * QUEUE, (index + 1) * QUEUE)
        messages[index, 0, :QUEUE] = mixed[part]
        messages[index, 0, QUEUE:] = grad_out[part]


def chunk_block(slots, rows, width, chunk):
    return pl.BlockSpec((slots, 1, rows, width), lambda i: (0, chunk, 0, 0))


def mixing_part(chunk, control, members, cotangents, previous):
    slots, chunks, share, _ = cotangents.shape
    width, columns = control.shape
    kernel = functools.partial(mixing_kernel, slots)
    ins = [control, members, cotangents]
    specs = [whole(width, columns), whole(LONG, width), chunk_block(slots, share, width, chunk)]
    aliases = {}
    if previous is not None:
        aliases = {len(ins): 1}
        kernel = without_previous(kernel, len(ins))
        ins.append(previous)
        specs.append(pl.BlockSpec(memory_space=pl.ANY))
    return call(
        kernel,
        f"mixing_{chunk}",
        (1,),
        specs,
        [whole(LONG, columns), chunk_block(slots, 2 * QUEUE, width, chunk)],
        [shape((LONG, columns), F32), shape((slots, chunks, 2 * QUEUE, width), BF)],
        (),
        (6 * LONG * columns * width, 4e6, LONG * columns),
        aliases,
    )(*ins)


def expert_kernel(slots, messages, w_expand, b_expand, w_reduce, b_reduce, *refs):
    answers, taken, grads, activated_out, grad_pre_out, out_sum, mixed_sum = refs
    step = pl.program_id(0)

    @pl.when(step == 0)
    def _():
        for index in range(slots):
            begin = 2 * QUEUE * index
            part = slice(index * QUEUE, (index + 1) * QUEUE)
            taken[part] = messages[begin : begin + QUEUE]
            grads[part] = messages[begin + QUEUE : begin + 2 * QUEUE]
        out_sum[...] = jnp.zeros_like(out_sum)
        mixed_sum[...] = jnp.zeros_like(mixed_sum)

    pre = dot(taken[...], w_expand[0]) + b_expand[...]
    slope = 0.7978845608028654
    square = pre * pre
    bend = jnp.tanh(slope * (pre + 0.044715 * (pre * square)))
    half = 0.5 * (1.0 + bend)
    activated = (pre * half).astype(BF)
    activated_out[...] = activated
    out_sum[...] += dot(activated, w_reduce[0])
    derivative = half + (0.5 * slope) * pre * (1.0 - bend * bend) * (1.0 + 0.134145 * square)
    grad_pre = (dot_cols(grads[...], w_reduce[0]) * derivative).astype(BF)
    grad_pre_out[...] = grad_pre
    mixed_sum[...] += dot_cols(grad_pre, w_expand[0])

    @pl.when(step == pl.num_programs(0) - 1)
    def _():
        for index in range(slots):
            begin = 2 * QUEUE * index
            part = slice(index * QUEUE, (index + 1) * QUEUE)
            answers[begin : begin + QUEUE] = (out_sum[part] + b_reduce[...]).astype(BF)
            answers[begin + QUEUE : begin + 2 * QUEUE] = mixed_sum[part].astype(BF)


def expert_part(messages, w_expand, b_expand, w_reduce, b_reduce):
    _, width, hidden = w_expand.shape
    count = messages.shape[0] // 2
    slots = count // QUEUE
    cut = min(512, hidden)
    outs = call(
        functools.partial(expert_kernel, slots),
        "expert",
        (hidden // cut,),
        [
            whole(2 * count, width),
            pl.BlockSpec((1, width, cut), lambda i: (0, 0, i)),
            pl.BlockSpec((1, cut), lambda i: (0, i)),
            pl.BlockSpec((1, cut, width), lambda i: (0, i, 0)),
            whole(1, width),
        ],
        [
            whole(2 * count, width),
            whole(count, width),
            whole(count, width),
            pl.BlockSpec((count, cut), lambda i: (0, i)),
            pl.BlockSpec((count, cut), lambda i: (0, i)),
        ],
        [shape((2 * count, width), BF)]
        + [shape((count, width), BF)] * 2
        + [shape((count, hidden), BF)] * 2,
        [pltpu.VMEM((count, width), F32), pltpu.VMEM((count, width), F32)],
        (8 * count * width * hidden, 8e6, count * hidden),
    )(messages, w_expand, b_expand, w_reduce, b_reduce)
    return outs[0], outs[1:]


def expert_weights_kernel(chunks, place, *refs):
    taken = refs[:chunks]
    grads = refs[chunks : 2 * chunks]
    activated = refs[2 * chunks : 3 * chunks]
    grad_pre = refs[3 * chunks : 4 * chunks]
    own, other, bias_e, bias_r, full_e, full_r = refs[4 * chunks :]
    join = lambda parts: jnp.concatenate([part[...] for part in parts], axis=0)
    pre = join(grad_pre)
    cotangent = join(grads)
    full_e[...] = dot_rows(join(taken), pre).astype(BF)
    full_r[...] = dot_rows(join(activated), cotangent).astype(BF)
    bias_e[...] = jnp.sum(pre.astype(F32), axis=0, keepdims=True)
    bias_r[...] = jnp.sum(cotangent.astype(F32), axis=0, keepdims=True)
    begin = 0
    for full in (full_e, full_r):
        cut = full.shape[0] // 2
        for out, side in ((own, place[1] % 2), (other, 1 - place[1] % 2)):
            out[begin : begin + cut] = full[pl.ds(pl.multiple_of(side * cut, cut), cut), :]
        begin += cut


def expert_weights(place, saved):
    chunks = len(saved)
    taken, grads, activated, grad_pre = zip(*saved)
    count, width = taken[0].shape
    hidden = activated[0].shape[1]
    cut = width
    steps = hidden // cut
    wide = lambda rows: pl.BlockSpec((rows, cut), lambda i: (0, i))
    tall = pl.BlockSpec((cut, width), lambda i: (i, 0))
    return call(
        functools.partial(expert_weights_kernel, chunks),
        "expert_weights",
        (steps,),
        [scalars()] + [whole(count, width)] * (2 * chunks) + [wide(count)] * (2 * chunks),
        [tall, tall, wide(1), whole(1, width)],
        [shape((hidden, width), BF)] * 2 + [shape((1, hidden), F32), shape((1, width), F32)],
        [pltpu.VMEM((width, cut), BF), pltpu.VMEM((cut, width), BF)],
        (4 * chunks * count * width * hidden, 9e6, 0),
    )(place, *taken, *grads, *activated, *grad_pre)


def place_weights_kernel(place, own, own_across, other, other_across, out_e, out_r):
    begin = 0
    for out in (out_e, out_r):
        cut = out.shape[1] // 2
        part = slice(begin, begin + cut)
        for one, two, side in (
            (own, own_across, place[1] % 2),
            (other, other_across, 1 - place[1] % 2),
        ):
            total = one[part].astype(F32) + two[part].astype(F32)
            out[0, pl.ds(pl.multiple_of(side * cut, cut), cut), :] = total
        begin += cut


def place_weights(place, *parts):
    hidden, width = parts[0].shape
    cut = width
    tall = pl.BlockSpec((cut, width), lambda i: (i, 0))
    return call(
        place_weights_kernel,
        "place_expert_weights",
        (hidden // cut,),
        [scalars()] + [tall] * len(parts),
        [
            pl.BlockSpec((1, width, cut), lambda i: (0, 0, i)),
            pl.BlockSpec((1, cut, width), lambda i: (0, i, 0)),
        ],
        [shape((1, width, hidden), F32), shape((1, hidden, width), F32)],
        cost=(0, 16 * width * hidden, 0),
    )(place, *parts)


def unmix_kernel(slots, control, mixing_ref, members, cotangents, answers, back, merged, control_out):
    rows = members[...]
    grads = cotangents[...].reshape(rows.shape)
    pick = lambda part: jnp.concatenate([answers[index, 0, part] for index in range(slots)], axis=0)
    expert_out, grad_mixed = pick(slice(0, QUEUE)), pick(slice(QUEUE, 2 * QUEUE))
    mixing = mixing_ref[...]
    low = mixing.astype(BF)
    grad_mixing = dot_cols(grads, expert_out) + dot_cols(rows, grad_mixed)
    weighted = mixing * grad_mixing
    grad_logits = weighted - mixing * jnp.sum(weighted, axis=0, keepdims=True)
    grad_logits = grad_logits.astype(BF)
    back[...] = (dot(low, grad_mixed) + dot_cols(grad_logits, control[...])).astype(BF)
    merged[...] = dot(low, expert_out).astype(BF).reshape(merged.shape)
    grad_control = dot_rows(grad_logits, rows)
    for index in range(slots):
        control_out[index : index + 1, :] = jnp.sum(
            grad_control[index * QUEUE : (index + 1) * QUEUE], axis=0, keepdims=True
        )


def without_previous(kernel, position):
    def inner(*refs):
        return kernel(*refs[:position], *refs[position + 1 :])

    return inner


def unmix_part(chunk, control, mixing, members, cotangents, answers, previous):
    slots, chunks, _, width = answers.shape
    columns = control.shape[1]
    share = LONG // slots
    kernel = functools.partial(unmix_kernel, slots)
    ins = [control, mixing, members, cotangents, answers]
    specs = [
        whole(width, columns),
        whole(LONG, columns),
        whole(LONG, width),
        chunk_block(slots, share, width, chunk),
        chunk_block(slots, 2 * QUEUE, width, chunk),
    ]
    aliases = {}
    if previous is not None:
        aliases = {len(ins): 1}
        kernel = without_previous(kernel, len(ins))
        ins.append(previous)
        specs.append(pl.BlockSpec(memory_space=pl.ANY))
    return call(
        kernel,
        f"unmix_{chunk}",
        (1,),
        specs,
        [whole(LONG, width), chunk_block(slots, share, width, chunk), whole(slots, width)],
        [
            shape((LONG, width), BF),
            shape((slots, chunks, share, width), BF),
            shape((slots, width), F32),
        ],
        (),
        (12 * LONG * columns * width, 6e6, 0),
        aliases,
    )(*ins)


def output_kernel(chunks, *refs):
    merged, out = refs[chunks:]
    for chunk in range(chunks):
        rows = merged[:, chunk].reshape(LONG, out.shape[1]).astype(F32)
        out[chunk * LONG : (chunk + 1) * LONG] = (refs[chunk][...] + rows).astype(BF)


def output_part(resids, merged):
    slots, chunks, share, width = merged.shape
    return call(
        functools.partial(output_kernel, chunks),
        "output",
        (1,),
        [whole(LONG, width)] * chunks + [whole(slots, chunks, share, width)],
        whole(chunks * LONG, width),
        shape((chunks * LONG, width), BF),
        cost=(0, 8e6, 0),
    )(*resids, merged)


def backward_kernel(pairs, begins, later, *refs):
    refs = list(refs)
    take = lambda count: [refs.pop(0) for _ in range(count)]
    if begins:
        back, resid, grad_output, gain_second = take(4)
    else:
        (resid_low,) = take(1)
    parts = take(len(pairs))
    normed, qkv, exps, inverse, attended = take(5)
    weights_before = take(len(pairs)) if later else None
    weights_out = take(len(pairs))
    (grads_out,) = take(1)
    if begins:
        gains_out, grad_resid, resid_low = take(3)
    normed_turned, w_now, o_now, queries_sum, keys_turned, values_turned = take(6)
    step = pl.program_id(0)
    pair_width = attended.shape[2]
    tiles = LONG // TILE

    @pl.when(step == 0)
    def _():
        normed_turned[...] = normed[...].T
        if begins:
            unit, scaling = normalize(resid[...])
            through, gain_grad = normalize_back(
                back[...].astype(F32), gain_second[...], unit, scaling
            )
            gains_out[...] = gain_grad
            total = grad_output[...].astype(F32) + through
            grad_resid[...] = total
            resid_low[...] = total.astype(BF)

    load_weights(step, lambda index: index, parts, None, o_now)
    low = resid_low[...]
    grad_attended = dot_cols(low, o_now[...]).astype(BF)
    grad_out_weights = dot_rows(attended[0], low)
    wide = grad_attended.astype(F32)
    inverted = inverse[0]
    scaled = wide * inverted
    products = scaled * attended[0].astype(F32)
    scaled = scaled.astype(BF)
    low_half, high_half = halves(BF)
    low_wide, high_wide = halves(F32)
    queries = qkv[0, :, :pair_width] * BF(HEAD_DIM**-0.5)
    key_rows = qkv[0, :, pair_width : 2 * pair_width]
    value_rows = qkv[0, :, 2 * pair_width :]
    scaled_keys = key_rows * BF(HEAD_DIM**-0.5)
    queries_sum[...] = jnp.zeros_like(queries_sum)
    keys_turned[...] = jnp.zeros_like(keys_turned)
    values_turned[...] = jnp.zeros_like(values_turned)
    for head, (half, half_wide) in enumerate(((low_half, low_wide), (high_half, high_wide))):
        head_grads = scaled * half
        head_queries = queries * half
        head_keys = scaled_keys * half
        deltas = jnp.sum(products * half_wide, axis=1, keepdims=True)
        for row_tile in range(tiles):
            begin, extent = row_tile * TILE, (row_tile + 1) * TILE
            powers = jnp.concatenate(
                [exps[0, head, tile_slot(row_tile, col_tile)] for col_tile in range(row_tile + 1)],
                axis=1,
            )
            grad_probs = dot_cols(head_grads[begin:extent], value_rows[:extent])
            grad_scores = (powers.astype(F32) * (grad_probs - deltas[begin:extent])).astype(BF)
            queries_sum[begin:extent] += dot(grad_scores, head_keys[:extent])
            keys_turned[:, :extent] += dot_rows(head_queries[begin:extent], grad_scores)
            values_turned[:, :extent] += dot_rows(head_grads[begin:extent], powers)
    grads = jnp.concatenate(
        [queries_sum[...].astype(BF), keys_turned[...].T.astype(BF), values_turned[...].T.astype(BF)],
        axis=1,
    )
    grads_out[0] = grads
    grad_weights = dot(normed_turned[...], grads)
    width = normed.shape[1]
    blocks = [grad_weights[:, index * pair_width : (index + 1) * pair_width] for index in range(3)]
    blocks += [
        grad_out_weights[:, index * pair_width : (index + 1) * pair_width]
        for index in range(width // pair_width)
    ]
    for index, out in enumerate(weights_out):

        @pl.when(step == index)
        def _(index=index, out=out):
            begin = 0
            for block in blocks:
                extent = begin + block.shape[0]
                if later:
                    block = block + weights_before[index][begin:extent]
                out[begin:extent] = block.astype(out.dtype)
                begin = extent


def backward_part(chunk, pairs, start, low, parts, saved, before, last):
    exps = saved[2]
    width = saved[0].shape[1]
    packed, pair_width = parts[0].shape
    triple = 3 * pair_width
    kept = exps.shape[2]
    first = pairs[0]
    per_pair = lambda *dims: pl.BlockSpec((1,) + dims, lambda i: (first - i,) + (0,) * len(dims))
    rows = whole(LONG, width)
    begins, later = start is not None, before is not None
    if begins:
        ins = [*start]
        specs = [rows, rows, pl.BlockSpec((LONG, width), lambda i: (chunk, 0)), whole(1, width)]
    else:
        ins, specs = [low], [rows]
    ins += [parts[pair] for pair in pairs] + list(saved)
    specs += [whole(packed, pair_width)] * len(pairs)
    specs += [
        rows,
        per_pair(LONG, triple),
        per_pair(2, kept, TILE, TILE),
        per_pair(LONG, pair_width),
        per_pair(LONG, pair_width),
    ]
    if later:
        ins += [before[pair] for pair in pairs]
        specs += [whole(packed, pair_width)] * len(pairs)
    out_specs = [whole(packed, pair_width)] * len(pairs)
    outs = [shape((packed, pair_width), BF if last else F32)] * len(pairs)
    out_specs.append(pl.BlockSpec((1, LONG, triple), lambda i: (i, 0, 0)))
    outs.append(shape((len(pairs), LONG, triple), BF))
    if begins:
        out_specs += [whole(1, width), rows, rows]
        outs += [shape((1, width), F32), shape((LONG, width), F32), shape((LONG, width), BF)]
    results = call(
        functools.partial(backward_kernel, pairs, begins, later),
        f"backward_{chunk}_{first}",
        (len(pairs),),
        specs,
        out_specs,
        outs,
        [
            pltpu.VMEM((width, LONG), BF),
            pltpu.VMEM((width, triple), BF),
            pltpu.VMEM((pair_width, width), BF),
            pltpu.VMEM((LONG, pair_width), F32),
            pltpu.VMEM((pair_width, LONG), F32),
            pltpu.VMEM((pair_width, LONG), F32),
        ],
        (6e9 * len(pairs), 6e6 * len(pairs), 0),
    )(*ins)
    count = len(pairs)
    return dict(zip(pairs, results[:count])), results[count], results[count + 1 :]


def finish_kernel(groups, *refs):
    chunks = len(groups)
    refs = list(refs)
    take = lambda count: [refs.pop(0) for _ in range(count)]
    tokens, gain_first = take(2)
    parts = take(sum(len(group) for group in groups[0]))
    grads = [take(len(groups[chunk])) for chunk in range(chunks)]
    resids = take(chunks)
    grad_tokens, gain_out, weights = refs
    step = pl.program_id(0)
    width = tokens.shape[1]
    pairs, triple = len(parts), weights.shape[1] // len(parts)

    @pl.when(step == 0)
    def _():
        gain_out[...] = jnp.zeros_like(gain_out)
        for pair, part in enumerate(parts):
            cut = triple // 3
            for block in range(3):
                begin = pair * triple + block * cut
                weights[:, begin : begin + cut] = part[block * width : (block + 1) * width]

    for chunk in range(chunks):

        @pl.when(step == chunk)
        def _(chunk=chunk):
            columns = {}
            for group, ref in zip(groups[chunk], grads[chunk]):
                for index, pair in enumerate(group):
                    columns[pair] = ref[index]
            joined = jnp.concatenate([columns[pair] for pair in range(pairs)], axis=1)
            unit, scaling = normalize(tokens[...].astype(F32))
            through, gain_grad = normalize_back(
                dot_cols(joined, weights[...]), gain_first[...], unit, scaling
            )
            gain_out[...] += gain_grad
            grad_tokens[...] = resids[chunk][...] + through


def finish_part(tokens, gain_first, parts, groups, grads, resids):
    total, width = tokens.shape
    chunks = total // LONG
    packed, pair_width = parts[0].shape
    rows = pl.BlockSpec((LONG, width), lambda i: (i, 0))
    flat = [ref for chunk in grads for ref in chunk]
    return call(
        functools.partial(finish_kernel, groups),
        "finish",
        (chunks,),
        [rows, whole(1, width)]
        + [whole(packed, pair_width)] * len(parts)
        + [whole(*ref.shape) for ref in flat]
        + [whole(LONG, width)] * chunks,
        [rows, whole(1, width)],
        [shape((total, width), F32), shape((1, width), F32)],
        [pltpu.VMEM((width, 3 * pair_width * len(parts)), BF)],
        (2 * total * width * 3 * pair_width * len(parts), 2e7, 0),
    )(tokens, gain_first, *parts, *flat, *resids)


def tail_pack_kernel(*refs):
    total = refs[0][...].astype(F32)
    for part in refs[1:-1]:
        total = total + part[...].astype(F32)
    refs[-1][...] = total.astype(BF)


def tail_pack(parts):
    rows, cut = parts[0].shape
    return call(
        tail_pack_kernel,
        "tail_pack",
        (1,),
        [whole(rows, cut)] * len(parts),
        whole(rows, cut),
        shape((rows, cut), BF),
        cost=(0, 3e6, 0),
    )(*parts)


def tail_sum_kernel(slots, pieces, small, out):
    share, cut = pieces.shape[1:]
    total = pieces[0].astype(F32)
    for index in range(1, slots):
        total = total + pieces[index].astype(F32)
    total = total.astype(BF)
    packed = jnp.concatenate(
        [small[:, begin : begin + cut] for begin in range(0, small.shape[1], cut)], axis=0
    ).astype(BF)
    for index in range(slots):
        out[index, :share] = total
        out[index, share:] = packed


def tail_sum(pieces, small):
    slots, share, cut = pieces.shape
    count, width = small.shape
    rows = share + count * width // cut
    return call(
        functools.partial(tail_sum_kernel, slots),
        "tail_sum",
        (1,),
        [whole(slots, share, cut), whole(count, width)],
        whole(slots, rows, cut),
        shape((slots, rows, cut), BF),
        cost=(0, 2e6, 0),
    )(pieces, small)


def gather_kernel(slots, share, pieces, *refs):
    outs, gain_first, gain_second, control, total = refs[:4], refs[4], refs[5], refs[6], refs[7]
    for index in range(slots):
        total[index * share : (index + 1) * share] = pieces[index, :share].astype(F32)
    cut = total.shape[1]
    begin = 0
    for out in outs[:3]:
        out[...] = total[begin : begin + out.shape[0]]
        begin += out.shape[0]
    last = outs[3]
    blocks = last.shape[1] // cut
    for index in range(blocks):
        last[:, index * cut : (index + 1) * cut] = total[begin : begin + last.shape[0]]
        begin += last.shape[0]
    small = pieces[0, share:].astype(F32)
    for index in range(1, slots):
        small = small + pieces[index, share:].astype(F32)
    count = small.shape[0] // blocks
    small = jnp.concatenate(
        [small[index * count : (index + 1) * count] for index in range(blocks)], axis=1
    )
    experts = control.shape[1]
    gain_first[...] = small[experts : experts + 1]
    gain_second[...] = small[experts + 1 : experts + 2]
    control[...] = small[:experts].T


def gather_weights(pieces, share, width, experts):
    slots, _, cut = pieces.shape
    outs = [(width, cut)] * 3 + [(cut, width), (1, width), (1, width), (width, experts)]
    return call(
        functools.partial(gather_kernel, slots, share),
        "gather_weights",
        (1,),
        [whole(*pieces.shape)],
        [whole(*dims) for dims in outs],
        [shape(dims, F32) for dims in outs],
        [pltpu.VMEM((share * slots, cut), F32)],
        (0, 3e6, 0),
    )(pieces)


def partner(value, axis, offset):
    count = lax.axis_size(axis)
    return lax.ppermute(value, axis, [(index, index ^ offset) for index in range(count)])


def exchange(value, axis):
    return lax.all_to_all(value, axis, 0, 0, tiled=True)


def tree_sum(parts):
    while len(parts) > 1:
        parts = [parts[index] + parts[index + 1] for index in range(0, len(parts), 2)]
    return parts[0]


def gather_head(part):
    sibling = partner(part, "head", 1)
    across = partner(part, "head", 2)
    return [part, sibling, across, partner(across, "head", 1)]


def add_low(*parts):
    return sum(part.astype(F32) for part in parts).astype(BF)


def after(value, *earlier):
    return lax.optimization_barrier((value, *earlier))[0]


def body(
    tokens,
    gain_first,
    w_query,
    w_key,
    w_value,
    w_out,
    gain_second,
    w_control,
    w_expand,
    b_expand,
    w_reduce,
    b_reduce,
    lengths,
    grad_output,
):
    rows_local, width = tokens.shape
    pair_width = w_query.shape[1]
    slots = lax.axis_size("seq")
    chunks = rows_local // LONG
    place = jnp.stack([lax.axis_index("seq"), lax.axis_index("head")]).astype(jnp.int32)
    gain_first = gain_first[None]
    gain_second = gain_second[None]
    parts = gather_head(pack_weights(w_query, w_key, w_value, w_out))
    experts = w_control.shape[1]
    control = jnp.repeat(w_control, QUEUE, axis=1)
    cotangents = exchange(pack_rows(grad_output, slots), "seq")

    forwards, members = [], []
    for chunk in range(chunks):
        *saved, second = forward_part(
            chunk, place, lengths, tokens, gain_first, parts, gain_second
        )
        forwards.append(saved)
        second = after(second, cotangents)
        members.append(exchange(second, "seq"))
    mixings, messages = [], None
    for chunk in range(chunks):
        mixing, messages = mixing_part(
            chunk, control, members[chunk], cotangents, messages
        )
        mixings.append(mixing)
    messages = exchange(messages, "seq")
    replies, kept = expert_part(
        messages.reshape(-1, width), w_expand, b_expand, w_reduce, b_reduce
    )
    answers = exchange(replies.reshape(messages.shape), "seq")
    backs, merged, controls = [], None, []
    for chunk in range(chunks):
        back, merged, grad_control = unmix_part(
            chunk, control, mixings[chunk], members[chunk], cotangents, answers, merged
        )
        backs.append(exchange(back, "seq"))
        controls.append(grad_control)

    own, other, bias_e, bias_r = expert_weights(place, [kept])
    own = add_low(own, partner(other, "head", 1))
    across = partner(own, "head", 2)
    placed = (own, across, partner(own, "head", 1), partner(across, "head", 1))

    pairs = tuple(reversed(range(len(parts))))
    early, late = pairs[: len(pairs) // 2], pairs[len(pairs) // 2 :]
    before, gains, groups, grads, resids = None, [], [], [], []
    for chunk in range(chunks):
        *saved, resid = forwards[chunk]
        back = backs[chunk]
        if chunk == chunks - 1:
            if gains:
                merged = after(merged, gains[-1])
            merged = exchange(merged, "seq")
            back = after(back, across)
            start = (back, resid, grad_output, gain_second)
            first_weights, first_grads, (gain, grad_resid, low) = backward_part(
                chunk, early, start, None, parts, saved, before, True
            )
            pieces = [partner(first_weights[pair], "head", pair) for pair in early]
            second_weights, second_grads, _ = backward_part(
                chunk, late, None, low, parts, saved, before, True
            )
            groups.append((early, late))
            grads.append((first_grads, second_grads))
        else:
            start = (back, resid, grad_output, gain_second)
            before, chunk_grads, (gain, grad_resid, low) = backward_part(
                chunk, pairs, start, None, parts, saved, before, False
            )
            groups.append((pairs,))
            grads.append((chunk_grads,))
        gains.append(gain)
        resids.append(grad_resid)
    resids[-1] = after(resids[-1], *pieces)
    grad_tokens, gain = finish_part(tokens, gain_first, parts, groups, grads, resids)

    pieces += [partner(second_weights[pair], "head", pair) for pair in late if pair]
    packed = tail_pack([second_weights[0]] + pieces)
    packed = after(packed, merged, *placed)
    pieces = exchange(packed, "seq").reshape(slots, -1, pair_width)

    hidden_rows = bias_e.shape[1] // width
    small = [sum(controls), gain, sum(gains), bias_e.reshape(-1, width), bias_r]
    used = experts + 3 + hidden_rows
    small = jnp.concatenate(small + [jnp.zeros((-used % 8, width), F32)], axis=0)
    small = tree_sum([small] + [partner(small, "head", index) for index in range(1, len(parts))])
    sent = -(-(experts + 2) // 8) * 8
    pieces = exchange(tail_sum(pieces, small[:sent]), "seq")
    share = parts[0].shape[0] // slots
    *weights, gain_first, gain_second, control = gather_weights(pieces, share, width, experts)
    grad_query, grad_key, grad_value, grad_w_out = weights
    grad_expand, grad_reduce = place_weights(place, *placed)
    output = output_part([saved[5] for saved in forwards], merged)
    after_gains = experts + 2
    return (
        output,
        grad_tokens,
        gain_first[0],
        grad_query,
        grad_key,
        grad_value,
        grad_w_out,
        gain_second[0],
        control,
        grad_expand,
        small[after_gains : after_gains + hidden_rows].reshape(1, -1),
        grad_reduce,
        small[after_gains + hidden_rows : used],
    )


def solution(mesh):
    in_specs = (
        P(("seq", "head"), None),
        P(),
        P(None, "head"),
        P(None, "head"),
        P(None, "head"),
        P("head", None),
        P(),
        P(),
        P("seq", None, None),
        P("seq", None),
        P("seq", None, None),
        P("seq", None),
        P("seq", None),
        P(("seq", "head"), None),
    )
    out_specs = (
        P(("seq", "head"), None),
        P(("seq", "head"), None),
        P(),
        P(None, "head"),
        P(None, "head"),
        P(None, "head"),
        P("head", None),
        P(),
        P(),
        P("seq", None, None),
        P("seq", None),
        P("seq", None, None),
        P("seq", None),
    )
    return jax.shard_map(body, mesh=mesh, in_specs=in_specs, out_specs=out_specs, check_vma=False)
```

profile of v0, /device:TPU:0, one launch (start us, length us, event | category | flops | bytes accessed | tf_op | source)
XLA Modules:
  0.0 384.2 jit_solution(6392692672265889464)
XLA Ops:
  0.6 3.0 pack_cotangent.1
  3.7 7.3 %all-to-all-start = ((bf16[8,2,128,512]{3,2,1,0:T(8,128)(2,1)}), bf16[8,2,128,512]{3,2,1,0:T(8,128)(2,1)}, u32[]{:S(2)}, u32[]{:S(2)}) async-start(bf16[8,2,128,512]{3,2,1,0:T(8,128)(2,1)} %pack_cotangent.1), calls=%async_computation | async-start | bytes 4194304 | tf_op jit(solution)/shard_map/all_to_all | solution.py:858
  11.0 1.9 pack_weights.1.refs_4_.refs_7_.refs_2_
  12.9 1.5 collective-permute-start.1
  14.4 12.1 %collective-permute-done.1.refs_6_.refs_5_.refs_4_ = bf16[2048,128]{1,0:T(8,128)(2,1)S(1)} collective-permute-done((bf16[2048,128]{1,0:T(8,128)(2,1)}, bf16[2048,128]{1,0:T(8,128)(2,1)S(1)}, u32[]{:S(2)}, u32[]{:S(2)}) %collective-permute-start.1) | collective-permute-done | bytes 524320 | tf_op jit(solution)/shard_map/ppermute | solution.py:854
  26.5 0.7 pad_add_fusion.refs_0_.place
  27.2 1.2 collective-permute-done.2.refs_7_.refs_4_.refs_5_
  28.4 0.8 copy-done.8
  29.2 22.9 %forward_0.1 = (bf16[1024,512]{1,0:T(8,128)(2,1)}, bf16[4,1024,384]{2,1,0:T(8,128)(2,1)}, bf16[4,2,10,256,256]{4,3,2,1,0:T(8,128)(2,1)}, f32[4,1024,128]{2,1,0:T...) custom-call(s32[2]{0:T(128)} %pad_add_fusion.refs_0_.place, ...), custom_call_target="tpu_custom_call" | custom-call | flops 10000000000 | bytes 25000000 | tf_op jit(solution)/shard_map/forward_0/pallas_call | solution.py:198
  52.1 7.2 %all-to-all-done.cotangents.refs_2_.refs_3_ = bf16[8,2,128,512]{3,2,1,0:T(8,128)(2,1)} async-done(((bf16[8,2,128,512]{3,2,1,0:T(8,128)(2,1)}), bf16[8,2,128,512]{3,2,1,0:T(8,128)(2,1)}, u32[]{:S(2)}, u32[]{:S(2)}) %all-to-all-start) | async-done | bytes 2097184 | tf_op jit(solution)/shard_map/all_to_all | solution.py:858
  59.3 3.8 all-to-all-start.2
  63.2 23.0 %forward_1.1 = (bf16[1024,512]{1,0:T(8,128)(2,1)}, bf16[4,1024,384]{2,1,0:T(8,128)(2,1)}, bf16[4,2,10,256,256]{4,3,2,1,0:T(8,128)(2,1)}, f32[4,1024,128]{2,1,0:T...) custom-call(s32[2]{0:T(128)} %pad_add_fusion.refs_0_.place, ...), custom_call_target="tpu_custom_call" | custom-call | flops 10000000000 | bytes 25000000 | tf_op jit(solution)/shard_map/forward_1/pallas_call | solution.py:198
  86.2 2.9 all-to-all-done.2
  89.1 1.0 copy-done.1
  90.0 3.6 all-to-all-start.1
  93.7 0.8 copy.34.control.refs_0_
  94.6 4.4 %mixing_0.1 = (f32[1024,256]{1,0:T(8,128)}, bf16[8,2,64,512]{3,2,1,0:T(8,128)(2,1)}) custom-call(bf16[512,256]{1,0:T(8,128)(2,1)} %copy.34.control.refs_0_, bf16[1024,512]{1,0:T(8,128)(2,1)} %bitcast.24, bf16[8,2,128,512]{3,2,1,0:T(8,128)(2,1)} %all-to-all-done.cotangents.refs_2_.refs_3_), custom_call_target="tpu_custom_call" | custom-call | flops 805306368 | bytes 4000000 | tf_op jit(solution)/shard_map/mixing_0/pallas_call | solution.py:317
  99.0 20.7 %all-to-all-done.1 = bf16[8,128,512]{2,1,0:T(8,128)(2,1)S(1)} async-done(((bf16[8,128,512]{2,1,0:T(8,128)(2,1)}), bf16[8,128,512]{2,1,0:T(8,128)(2,1)S(1)}, u32[]{:S(2)}, u32[]{:S(2)}) %all-to-all-start.1) | async-done | bytes 1048608 | tf_op jit(solution)/shard_map/all_to_all | solution.py:858
  119.6 1.0 copy-done
  120.6 4.4 %mixing_1.1 = (f32[1024,256]{1,0:T(8,128)}, bf16[8,2,64,512]{3,2,1,0:T(8,128)(2,1)}) custom-call(bf16[512,256]{1,0:T(8,128)(2,1)} %copy.34.control.refs_0_, bf16[1024,512]{1,0:T(8,128)(2,1)} %bitcast.22, bf16[8,2,128,512]{3,2,1,0:T(8,128)(2,1)} %all-to-all-done.cotangents.refs_2_.refs_3_, ...), custom_call_target="tpu_custom_call", output_to_operand_aliasing={{1}: (3, {})} | custom-call | flops 805306368 | bytes 4000000 | tf_op jit(solution)/shard_map/mixing_1/pallas_call | solution.py:317
  125.0 29.7 %all_to_all.79 = bf16[8,2,64,512]{3,2,1,0:T(8,128)(2,1)} all-to-all(bf16[8,2,64,512]{3,2,1,0:T(8,128)(2,1)} %get-tuple-element.87), channel_id=1, replica_groups=mesh['seq'=8,'head'=4] {'seq'}, dimensions={0} | all-to-all | bytes 2097152 | tf_op jit(solution)/shard_map/all_to_all | solution.py:858
  154.7 9.9 %expert.1 = (bf16[1024,512]{1,0:T(8,128)(2,1)}, bf16[512,512]{1,0:T(8,128)(2,1)}, bf16[512,512]{1,0:T(8,128)(2,1)}, bf16[512,2048]{1,0:T(8,128)(2,1)}, bf16[512,2048]{1,0:T(8,128)(2,1)}) custom-call(bf16[1024,512]{1,0:T(8,128)(2,1)} %bitcast.32, bf16[1,512,2048]{2,1,0:T(8,128)(2,1)} %w_expand.1, f32[1,2048]{1,0:T(1,128)} %b_expand.1, ...), custom_call_target="tpu_custom_call" | custom-call | flops 4294967296 | bytes 8000000 | tf_op jit(solution)/shard_map/expert/pallas_call | solution.py:371
  164.6 3.8 all-to-all-start.4
  168.4 6.8 %expert_weights.1 = (bf16[2048,512]{1,0:T(8,128)(2,1)}, bf16[2048,512]{1,0:T(8,128)(2,1)}, f32[1,2048]{1,0:T(1,128)}, f32[1,512]{1,0:T(1,128)}) custom-call(s32[2]{0:T(128)} %pad_add_fusion.refs_0_.place, bf16[512,512]{1,0:T(8,128)(2,1)} %get-tuple-element.102.refs_0_, bf16[512,512]{1,0:T(8,128)(2,1)} %get-tuple-element.103.refs_1_, ...), custom_call_target="tpu_custom_call" | custom-call | flops 2147483648 | bytes 9000000 | tf_op jit(solution)/shard_map/expert_weights/pallas_call | solution.py:428
  175.2 18.7 %all-to-all-done.4.answers.refs_4_ = bf16[8,2,64,512]{3,2,1,0:T(8,128)(2,1)S(1)} async-done(((bf16[8,2,64,512]{3,2,1,0:T(8,128)(2,1)}), bf16[8,2,64,512]{3,2,1,0:T(8,128)(2,1)S(1)}, u32[]{:S(2)}, u32[]{:S(2)}) %all-to-all-start.4) | async-done | bytes 1048608 | tf_op jit(solution)/shard_map/all_to_all | solution.py:858
  193.9 1.0 copy-done.2
  194.9 6.1 %unmix_0.1 = (bf16[1024,512]{1,0:T(8,128)(2,1)}, bf16[8,2,128,512]{3,2,1,0:T(8,128)(2,1)}, f32[8,512]{1,0:T(8,128)}) custom-call(bf16[512,256]{1,0:T(8,128)(2,1)} %copy.34.control.refs_0_, f32[1024,256]{1,0:T(8,128)} %get-tuple-element.89.mixing_ref, bf16[1024,512]{1,0:T(8,128)(2,1)} %bitcast.25, ...), custom_call_target="tpu_custom_call" | custom-call | flops 1610612736 | bytes 6000000 | tf_op jit(solution)/shard_map/unmix_0/pallas_call | solution.py:518
  201.0 3.6 all-to-all-start.5
  204.5 6.1 %unmix_1.1 = (bf16[1024,512]{1,0:T(8,128)(2,1)}, bf16[8,2,128,512]{3,2,1,0:T(8,128)(2,1)}, f32[8,512]{1,0:T(8,128)}) custom-call(bf16[512,256]{1,0:T(8,128)(2,1)} %copy.34.control.refs_0_, f32[1024,256]{1,0:T(8,128)} %get-tuple-element.86.refs_1_, bf16[1024,512]{1,0:T(8,128)(2,1)} %bitcast.23, ...), custom_call_target="tpu_custom_call", output_to_operand_aliasing={{1}: (5, {})} | custom-call | flops 1610612736 | bytes 6000000 | tf_op jit(solution)/shard_map/unmix_1/pallas_call | solution.py:518
  210.7 4.2 %add_convert_fusion.own = bf16[2048,512]{1,0:T(8,128)(2,1)} fusion(bf16[2048,512]{1,0:T(8,128)(2,1)} %collective-permute-done.3, bf16[2048,512]{1,0:T(8,128)(2,1)} %get-tuple-element.106), kind=kLoop, calls=%fused_computation | loop fusion | flops 4194304 | bytes 6291456 | tf_op jit(solution)/shard_map/convert_element_type | solution.py:874
  214.8 1.5 collective-permute-start.4
  216.3 14.0 %all-to-all-done.5 = bf16[8,128,512]{2,1,0:T(8,128)(2,1)S(1)} async-done(((bf16[8,128,512]{2,1,0:T(8,128)(2,1)}), bf16[8,128,512]{2,1,0:T(8,128)(2,1)S(1)}, u32[]{:S(2)}, u32[]{:S(2)}) %all-to-all-start.5) | async-done | bytes 1048608 | tf_op jit(solution)/shard_map/all_to_all | solution.py:858
  230.3 4.2 %all-to-all-start.7 = ((bf16[8,128,512]{2,1,0:T(8,128)(2,1)}), bf16[8,128,512]{2,1,0:T(8,128)(2,1)}, u32[]{:S(2)}, u32[]{:S(2)}) async-start(bf16[8,128,512]{2,1,0:T(8,128)(2,1)} %bitcast.13), calls=%async_computation.7 | async-start | bytes 2097152 | tf_op jit(solution)/shard_map/all_to_all | solution.py:858
  234.6 26.0 %backward_0_3.1 = (f32[2048,128]{1,0:T(8,128)}, f32[2048,128]{1,0:T(8,128)}, f32[2048,128]{1,0:T(8,128)}, f32[2048,128]{1,0:T(8,128)}, bf16[4,1024,384]{2,1,0:T(...) custom-call(bf16[1024,512]{1,0:T(8,128)(2,1)} %bitcast.27, ...), custom_call_target="tpu_custom_call" | custom-call | flops 24000000000 | bytes 24000000 | tf_op jit(solution)/shard_map/backward_0_3/pallas_call | solution.py:680
  260.5 6.3 %all-to-all-start.6 = ((bf16[8,2,128,512]{3,2,1,0:T(8,128)(2,1)}), bf16[8,2,128,512]{3,2,1,0:T(8,128)(2,1)}, u32[]{:S(2)}, u32[]{:S(2)}) async-start(bf16[8,2,128,512]{3,2,1,0:T(8,128)(2,1)} %get-tuple-element.99), calls=%async_computation.6 | async-start | bytes 4194304 | tf_op jit(solution)/shard_map/all_to_all | solution.py:858
  267.5 17.5 %backward_1_3.1 = (bf16[2048,128]{1,0:T(8,128)(2,1)}, bf16[2048,128]{1,0:T(8,128)(2,1)}, bf16[2,1024,384]{2,1,0:T(8,128)(2,1)}, f32[1,512]{1,0:T(1,128)}, f32[10...) custom-call(bf16[1024,512]{1,0:T(8,128)(2,1)} %bitcast.14.refs_0_, f32[1024,512]{1,0:T(8,128)} %get-tuple-element.80.refs_1_, ...), custom_call_target="tpu_custom_call" | custom-call | flops 12000000000 | bytes 12000000 | tf_op jit(solution)/shard_map/backward_1_3/pallas_call | solution.py:680
  284.9 13.9 %backward_1_1.1 = (bf16[2048,128]{1,0:T(8,128)(2,1)}, bf16[2048,128]{1,0:T(8,128)(2,1)}, bf16[2,1024,384]{2,1,0:T(8,128)(2,1)}) custom-call(bf16[1024,512]{1,0:T(8,128)(2,1)} %get-tuple-element.117.refs_0_, bf16[2048,128]{1,0:T(8,128)(2,1)} %copy-done.7, bf16[2048,128]{1,0:T(8,128)(2,1)} %pack_weights.1.refs_4_.refs_7_.refs_2_, ...), custom_call_target="tpu_custom_call" | custom-call | flops 12000000000 | bytes 12000000 | tf_op jit(solution)/shard_map/backward_1_1/pallas_call | solution.py:680
  299.0 1.5 collective-permute-start.5
  300.5 0.5 collective-permute-start.6
  301.1 12.0 %collective-permute-done.5.refs_1_ = bf16[2048,128]{1,0:T(8,128)(2,1)S(1)} collective-permute-done((bf16[2048,128]{1,0:T(8,128)(2,1)}, bf16[2048,128]{1,0:T(8,128)(2,1)S(1)}, u32[]{:S(2)}, u32[]{:S(2)}) %collective-permute-start.5) | collective-permute-done | bytes 524320 | tf_op jit(solution)/shard_map/ppermute | solution.py:854
  313.1 11.6 %collective-permute-done.6.refs_2_ = bf16[2048,128]{1,0:T(8,128)(2,1)S(1)} collective-permute-done((bf16[2048,128]{1,0:T(8,128)(2,1)}, bf16[2048,128]{1,0:T(8,128)(2,1)S(1)}, u32[]{:S(2)}, u32[]{:S(2)}) %collective-permute-start.6) | collective-permute-done | bytes 524320 | tf_op jit(solution)/shard_map/ppermute | solution.py:854
  324.7 0.8 copy-done.11
  325.5 2.6 tail_pack.1
  328.1 6.2 %all-to-all-start.8 = ((bf16[8,256,128]{2,1,0:T(8,128)(2,1)}), bf16[8,256,128]{2,1,0:T(8,128)(2,1)S(1)}, u32[]{:S(2)}, u32[]{:S(2)}) async-start(bf16[8,256,128]{2,1,0:T(8,128)(2,1)} %bitcast.26), calls=%async_computation.8 | async-start | bytes 1048576 | tf_op jit(solution)/shard_map/all_to_all | solution.py:858
  334.3 0.5 broadcast.3
  334.8 0.7 reduce.3
  335.6 11.7 %finish.1 = (f32[2048,512]{1,0:T(8,128)}, f32[1,512]{1,0:T(1,128)}) custom-call(bf16[2048,512]{1,0:T(8,128)(2,1)} %refs_0_.1, f32[1,512]{1,0:T(1,128)} %bitcast.37, bf16[2048,128]{1,0:T(8,128)(2,1)} %pack_weights.1.refs_4_.refs_7_.refs_2_, bf16[2048,128]{1,0:T(8,128)(2,1)} %copy-done.7, bf16[2048,128]{1,0:T(8,128)(2,1)} %copy-done.6, ...), custom_call_target="tpu_custom_call" | custom-call | flops 3221225472 | bytes 20000000 | tf_op jit(solution)/shard_map/finish/pallas_call | solution.py:746
  347.3 0.7 concatenate.3
  348.4 1.2 collective-permute-start.11
  349.9 1.8 collective-permute-done.12
  351.7 0.7 collective-permute-done.11
  352.4 0.6 add_add_fusion.small
  353.0 0.8 copy-done.4
  353.8 2.0 tail_sum.1
  355.8 5.7 %all-to-all-start.9 = ((bf16[8,320,128]{2,1,0:T(8,128)(2,1)}), bf16[8,320,128]{2,1,0:T(8,128)(2,1)S(1)}, u32[]{:S(2)}, u32[]{:S(2)}) async-start(bf16[8,320,128]{2,1,0:T(8,128)(2,1)} %tail_sum.1), calls=%async_computation.9 | async-start | bytes 1310720 | tf_op jit(solution)/shard_map/all_to_all | solution.py:858
  361.5 1.3 slice.9
  362.8 0.7 slice_bitcast_fusion
  363.5 0.6 copy.36
  364.1 7.0 %place_expert_weights.1 = (f32[1,512,2048]{2,1,0:T(8,128)}, f32[1,2048,512]{2,1,0:T(8,128)}) custom-call(s32[2]{0:T(128)} %pad_add_fusion.refs_0_.place, bf16[2048,512]{1,0:T(8,128)(2,1)} %add_convert_fusion.own, bf16[2048,512]{1,0:T(8,128)(2,1)} %collective-permute-done.4.own_across, bf16[2048,512]{1,0:T(8,128)(2,1)} %collective-permute-done.8.other, ...), custom_call_target="tpu_custom_call" | custom-call | bytes 16777216 | tf_op jit(solution)/shard_map/place_expert_weights/pallas_call | solution.py:458
  371.1 4.5 %output.1 = bf16[2048,512]{1,0:T(8,128)(2,1)} custom-call(f32[1024,512]{1,0:T(8,128)} %get-tuple-element.79.refs_1_.refs_0_, f32[1024,512]{1,0:T(8,128)} %get-tuple-element.80.refs_1_, bf16[8,2,128,512]{3,2,1,0:T(8,128)(2,1)} %all-to-all-done.6.refs_2_), custom_call_target="tpu_custom_call" | custom-call | bytes 8000000 | tf_op jit(solution)/shard_map/output/pallas_call | solution.py:544
  375.6 3.6 all-to-all-done.9.pieces
  379.3 0.8 copy-done.3
  380.1 2.2 gather_weights.1
  382.3 1.7 copy.35
  (54 shorter events, 1.6 us)
Async XLA Ops:
  3.7 55.6 %all-to-all-start = ((bf16[8,2,128,512]{3,2,1,0:T(8,128)(2,1)}), bf16[8,2,128,512]{3,2,1,0:T(8,128)(2,1)}, u32[]{:S(2)}, u32[]{:S(2)}) async-start(bf16[8,2,128,512]{3,2,1,0:T(8,128)(2,1)} %pack_cotangent.1), calls=%async_computation | async-start | bytes 4194304 | tf_op jit(solution)/shard_map/all_to_all | solution.py:858
  12.9 13.6 %collective-permute-start.1 = (bf16[2048,128]{1,0:T(8,128)(2,1)}, bf16[2048,128]{1,0:T(8,128)(2,1)S(1)}, u32[]{:S(2)}, u32[]{:S(2)}) collective-permute-start(bf16[2048,128]{1,0:T(8,128)(2,1)} %pack_weights.1.refs_4_.refs_7_.refs_2_), channel_id=1, source_target_pairs={{0,2},{1,3},{2,0},{3,1},{4,6},{5,7},{6,4},{7,5},{8,10},{9,11},{10,... | collective-permute-start | bytes 1572872 | tf_op jit(solution)/shard_map/ppermute | solution.py:854
  14.4 12.8 %collective-permute-start = (bf16[2048,128]{1,0:T(8,128)(2,1)}, bf16[2048,128]{1,0:T(8,128)(2,1)S(1)}, u32[]{:S(2)}, u32[]{:S(2)}) collective-permute-start(bf16[2048,128]{1,0:T(8,128)(2,1)} %pack_weights.1.refs_4_.refs_7_.refs_2_), channel_id=1, source_target_pairs={{0,1},{1,0},{2,3},{3,2},{4,5},{5,4},{6,7},{7,6},{8,9},{9,8},{10,11... | collective-permute-start | bytes 1572872 | tf_op jit(solution)/shard_map/ppermute | solution.py:854
  26.5 1.9 copy-start.6
  26.5 1.9 collective-permute-start.2
  27.2 1.2 copy-start.7
  28.4 0.8 copy-start.8
  59.3 29.7 %all-to-all-start.2 = ((bf16[8,128,512]{2,1,0:T(8,128)(2,1)}), bf16[8,128,512]{2,1,0:T(8,128)(2,1)S(1)}, u32[]{:S(2)}, u32[]{:S(2)}) async-start(bf16[8,128,512]{2,1,0:T(8,128)(2,1)} %bitcast.29), calls=%async_computation.2 | async-start | bytes 2097152 | tf_op jit(solution)/shard_map/all_to_all | solution.py:858
  86.1 7.5 %copy-start.14 = (bf16[512,8]{0,1:T(8,128)(2,1)S(1)}, bf16[512,8]{0,1:T(8,128)(2,1)}, u32[]{:S(2)}) copy-start(bf16[512,8]{0,1:T(8,128)(2,1)} %param.21) | copy-start | bytes 24580
  89.1 1.0 copy-start.1
  90.0 29.6 %all-to-all-start.1 = ((bf16[8,128,512]{2,1,0:T(8,128)(2,1)}), bf16[8,128,512]{2,1,0:T(8,128)(2,1)S(1)}, u32[]{:S(2)}, u32[]{:S(2)}) async-start(bf16[8,128,512]{2,1,0:T(8,128)(2,1)} %bitcast.30), calls=%async_computation.1 | async-start | bytes 2097152 | tf_op jit(solution)/shard_map/all_to_all | solution.py:858
  119.6 1.0 copy-start
  164.6 29.3 %all-to-all-start.4 = ((bf16[8,2,64,512]{3,2,1,0:T(8,128)(2,1)}), bf16[8,2,64,512]{3,2,1,0:T(8,128)(2,1)S(1)}, u32[]{:S(2)}, u32[]{:S(2)}) async-start(bf16[8,2,64,512]{3,2,1,0:T(8,128)(2,1)} %bitcast.31), calls=%async_computation.4 | async-start | bytes 2097152 | tf_op jit(solution)/shard_map/all_to_all | solution.py:858
  175.2 35.5 %collective-permute-start.3 = (bf16[2048,512]{1,0:T(8,128)(2,1)}, bf16[2048,512]{1,0:T(8,128)(2,1)}, u32[]{:S(2)}, u32[]{:S(2)}) collective-permute-start(bf16[2048,512]{1,0:T(8,128)(2,1)} %get-tuple-element.107), channel_id=1, source_target_pairs={{0,1},{1,0},{2,3},{3,2},{4,5},{5,4},{6,7},{7,6},{8,9},{9,8},{10,11... | collective-permute-start | bytes 6291464 | tf_op jit(solution)/shard_map/ppermute | solution.py:854
  193.9 1.0 copy-start.2
  201.0 29.3 %all-to-all-start.5 = ((bf16[8,128,512]{2,1,0:T(8,128)(2,1)}), bf16[8,128,512]{2,1,0:T(8,128)(2,1)S(1)}, u32[]{:S(2)}, u32[]{:S(2)}) async-start(bf16[8,128,512]{2,1,0:T(8,128)(2,1)} %bitcast.28), calls=%async_computation.5 | async-start | bytes 2097152 | tf_op jit(solution)/shard_map/all_to_all | solution.py:858
  214.8 52.1 %collective-permute-start.4 = (bf16[2048,512]{1,0:T(8,128)(2,1)}, bf16[2048,512]{1,0:T(8,128)(2,1)}, u32[]{:S(2)}, u32[]{:S(2)}) collective-permute-start(bf16[2048,512]{1,0:T(8,128)(2,1)} %add_convert_fusion.own), channel_id=1, source_target_pairs={{0,2},{1,3},{2,0},{3,1},{4,6},{5,7},{6,4},{7,5},{8,10},{9,11},{10,... | collective-permute-start | bytes 6291464 | tf_op jit(solution)/shard_map/ppermute | solution.py:854
  230.3 4.2 %copy-start.5 = (bf16[8,128,512]{2,1,0:T(8,128)(2,1)}, bf16[8,128,512]{2,1,0:T(8,128)(2,1)S(1)}, u32[]{:S(2)}) copy-start(bf16[8,128,512]{2,1,0:T(8,128)(2,1)S(1)} %all-to-all-done.5) | copy-start | bytes 3145732
  230.3 30.2 %all-to-all-start.7 = ((bf16[8,128,512]{2,1,0:T(8,128)(2,1)}), bf16[8,128,512]{2,1,0:T(8,128)(2,1)}, u32[]{:S(2)}, u32[]{:S(2)}) async-start(bf16[8,128,512]{2,1,0:T(8,128)(2,1)} %bitcast.13), calls=%async_computation.7 | async-start | bytes 2097152 | tf_op jit(solution)/shard_map/all_to_all | solution.py:858
  260.5 67.5 %all-to-all-start.6 = ((bf16[8,2,128,512]{3,2,1,0:T(8,128)(2,1)}), bf16[8,2,128,512]{3,2,1,0:T(8,128)(2,1)}, u32[]{:S(2)}, u32[]{:S(2)}) async-start(bf16[8,2,128,512]{3,2,1,0:T(8,128)(2,1)} %get-tuple-element.99), calls=%async_computation.6 | async-start | bytes 4194304 | tf_op jit(solution)/shard_map/all_to_all | solution.py:858
  266.9 61.2 %collective-permute-start.8 = (bf16[2048,512]{1,0:T(8,128)(2,1)}, bf16[2048,512]{1,0:T(8,128)(2,1)}, u32[]{:S(2)}, u32[]{:S(2)}) collective-permute-start(bf16[2048,512]{1,0:T(8,128)(2,1)} %add_convert_fusion.own), channel_id=1, source_target_pairs={{0,1},{1,0},{2,3},{3,2},{4,5},{5,4},{6,7},{7,6},{8,9},{9,8},{10,11... | collective-permute-start | bytes 6291464 | tf_op jit(solution)/shard_map/ppermute | solution.py:854
  267.0 61.1 %collective-permute-start.9 = (bf16[2048,512]{1,0:T(8,128)(2,1)}, bf16[2048,512]{1,0:T(8,128)(2,1)}, u32[]{:S(2)}, u32[]{:S(2)}) collective-permute-start(bf16[2048,512]{1,0:T(8,128)(2,1)} %collective-permute-done.4.own_across), channel_id=1, source_target_pairs={{0,1},{1,0},{2,3},{3,2},{4,5},{5,4},{6,7},{7,6},{8,9},{9,8},{10,11... | collective-permute-start | bytes 6291464 | tf_op jit(solution)/shard_map/ppermute | solution.py:854
  298.8 36.0 %copy-start.15 = (f32[1,2048]{1,0:T(1,128)S(1)}, f32[1,2048]{1,0:T(1,128)}, u32[]{:S(2)}) copy-start(f32[1,2048]{1,0:T(1,128)} %get-tuple-element.134) | copy-start | bytes 24580
  298.8 36.7 %copy-start.12 = (f32[8,512]{1,0:T(8,128)S(1)}, f32[8,512]{1,0:T(8,128)}, u32[]{:S(2)}) copy-start(f32[8,512]{1,0:T(8,128)} %get-tuple-element.130) | copy-start | bytes 49156
  298.8 36.7 %copy-start.13 = (f32[8,512]{1,0:T(8,128)S(1)}, f32[8,512]{1,0:T(8,128)}, u32[]{:S(2)}) copy-start(f32[8,512]{1,0:T(8,128)} %get-tuple-element.131) | copy-start | bytes 49156
  298.8 36.7 %copy-start.17 = (f32[1,512]{1,0:T(1,128)S(1)}, f32[1,512]{1,0:T(1,128)}, u32[]{:S(2)}) copy-start(f32[1,512]{1,0:T(1,128)} %get-tuple-element.98) | copy-start | bytes 6148
  298.9 36.7 %copy-start.18 = (f32[1,512]{1,0:T(1,128)S(1)}, f32[1,512]{1,0:T(1,128)}, u32[]{:S(2)}) copy-start(f32[1,512]{1,0:T(1,128)} %get-tuple-element.133) | copy-start | bytes 6148
  298.9 2.2 collective-permute-start.7
  299.0 14.1 %collective-permute-start.5 = (bf16[2048,128]{1,0:T(8,128)(2,1)}, bf16[2048,128]{1,0:T(8,128)(2,1)S(1)}, u32[]{:S(2)}, u32[]{:S(2)}) collective-permute-start(bf16[2048,128]{1,0:T(8,128)(2,1)} %get-tuple-element.123), channel_id=1, source_target_pairs={{0,3},{1,2},{2,1},{3,0},{4,7},{5,6},{6,5},{7,4},{8,11},{9,10},{10,... | collective-permute-start | bytes 1572872 | tf_op jit(solution)/shard_map/ppermute | solution.py:854
  300.5 24.1 %collective-permute-start.6 = (bf16[2048,128]{1,0:T(8,128)(2,1)}, bf16[2048,128]{1,0:T(8,128)(2,1)S(1)}, u32[]{:S(2)}, u32[]{:S(2)}) collective-permute-start(bf16[2048,128]{1,0:T(8,128)(2,1)} %get-tuple-element.124), channel_id=1, source_target_pairs={{0,2},{1,3},{2,0},{3,1},{4,6},{5,7},{6,4},{7,5},{8,10},{9,11},{10,... | collective-permute-start | bytes 1572872 | tf_op jit(solution)/shard_map/ppermute | solution.py:854
  301.1 23.6 %copy-start.9 = (bf16[2048,128]{1,0:T(8,128)(2,1)}, bf16[2048,128]{1,0:T(8,128)(2,1)S(1)}, u32[]{:S(2)}) copy-start(bf16[2048,128]{1,0:T(8,128)(2,1)S(1)} %collective-permute-done.7.refs_3_) | copy-start | bytes 1572868
  313.1 11.6 %copy-start.10 = (bf16[2048,128]{1,0:T(8,128)(2,1)}, bf16[2048,128]{1,0:T(8,128)(2,1)S(1)}, u32[]{:S(2)}) copy-start(bf16[2048,128]{1,0:T(8,128)(2,1)S(1)} %collective-permute-done.5.refs_1_) | copy-start | bytes 1572868
  324.7 0.8 copy-start.11
  328.1 25.0 %all-to-all-start.8 = ((bf16[8,256,128]{2,1,0:T(8,128)(2,1)}), bf16[8,256,128]{2,1,0:T(8,128)(2,1)S(1)}, u32[]{:S(2)}, u32[]{:S(2)}) async-start(bf16[8,256,128]{2,1,0:T(8,128)(2,1)} %bitcast.26), calls=%async_computation.8 | async-start | bytes 1048576 | tf_op jit(solution)/shard_map/all_to_all | solution.py:858
  335.6 11.7 %copy-start.16 = (f32[1,512]{1,0:T(1,128)S(1)}, f32[1,512]{1,0:T(1,128)}, u32[]{:S(2)}) copy-start(f32[1,512]{1,0:T(1,128)} %get-tuple-element.135) | copy-start | bytes 6148
  348.0 3.7 collective-permute-start.12
  348.4 4.0 %collective-permute-start.11 = (f32[16,512]{1,0:T(8,128)S(1)}, f32[16,512]{1,0:T(8,128)S(1)}, u32[]{:S(2)}, u32[]{:S(2)}) collective-permute-start(f32[16,512]{1,0:T(8,128)S(1)} %concatenate.3), channel_id=1, source_target_pairs={{0,2},{1,3},{2,0},{3,1},{4,6},{5,7},{6,4},{7,5},{8,10},{9,11},{10,... | collective-permute-start | bytes 98312 | tf_op jit(solution)/shard_map/ppermute | solution.py:854
  349.6 2.8 collective-permute-start.10
  353.0 0.8 copy-start.4
  355.8 23.5 %all-to-all-start.9 = ((bf16[8,320,128]{2,1,0:T(8,128)(2,1)}), bf16[8,320,128]{2,1,0:T(8,128)(2,1)S(1)}, u32[]{:S(2)}, u32[]{:S(2)}) async-start(bf16[8,320,128]{2,1,0:T(8,128)(2,1)} %tail_sum.1), calls=%async_computation.9 | async-start | bytes 1310720 | tf_op jit(solution)/shard_map/all_to_all | solution.py:858
  379.3 0.8 copy-start.3
where the time goes:
time: 391 us; the launch traced here: 384 us
  Pallas kernels  176 us (45%)
  waiting for transfers between devices  106 us (27%)
  starting transfers between devices  52.3 us (13%)
  blocking collectives  29.7 us (8%)
  local copies, waits for them, and re-layouts  12.6 us (3%)
  other arithmetic  6.13 us (2%)
    all_to_all x9, waiting for transfers between devices, exchange(): return lax.all_to_all(value, axis, 0, 0, tiled=True)  67 us
    pallas_call x3, Pallas kernels, backward_part(): call(functools.partial(backward_kernel, pairs, begins, later), f'backward...  57.3 us
    pallas_call x2, Pallas kernels, forward_part(): call(functools.partial(forward_kernel, pairs, chunk, rows // LONG), f'for...  45.9 us
    all_to_all x9, starting transfers between devices, exchange(): return lax.all_to_all(value, axis, 0, 0, tiled=True)  44.6 us
    ppermute x13, waiting for transfers between devices, partner(): lax.ppermute(value, axis, [(index, index ^ offset) for index in range(cou...  39.4 us
    all_to_all x1, blocking collectives, exchange(): return lax.all_to_all(value, axis, 0, 0, tiled=True)  29.7 us
    pallas_call x2, Pallas kernels, unmix_part(): call(kernel, f'unmix_{chunk}', (1,), specs, [whole(LONG, width), chunk_bl...  12.2 us
    pallas_call x1, Pallas kernels, finish_part(): call(functools.partial(finish_kernel, groups), 'finish', (chunks,), [rows...  11.7 us
  transfers between devices with their start and end apart: 22, of which 12 were waited for; matrix products, arithmetic and copies ran while one was open for 3% of the time, Pallas kernels for 40%

commit v1 on v0

--- a/solution.py
+++ b/solution.py
@@ -17,7 +17,8 @@
 F32 = jnp.float32
 ROWS_BY_ROWS = (((0,), (0,)), ((), ()))
 COLS_BY_COLS = (((1,), (1,)), ((), ()))
-VMEM_LIMIT = 62 * 1024 * 1024
+LARGE = 62 * 1024 * 1024
+SMALL = 28 * 1024 * 1024
 
 
 def dot(left, right):
@@ -57,7 +58,7 @@
     return pl.BlockSpec(memory_space=pltpu.SMEM)
 
 
-def call(kernel, name, grid, in_specs, out_specs, out_shape, scratch=(), cost=(0, 0, 0), aliases=None):
+def call(kernel, name, grid, in_specs, out_specs, out_shape, scratch=(), cost=(0, 0, 0), aliases=None, limit=SMALL):
     return pl.pallas_call(
         kernel,
         grid=grid,
@@ -69,7 +70,7 @@
         cost_estimate=pl.CostEstimate(
             flops=int(cost[0]), bytes_accessed=int(cost[1]), transcendentals=int(cost[2])
         ),
-        compiler_params=pltpu.CompilerParams(vmem_limit_bytes=VMEM_LIMIT),
+        compiler_params=pltpu.CompilerParams(vmem_limit_bytes=limit),
         name=name,
     )
 
@@ -88,35 +89,32 @@
     return first.astype(dtype), (1.0 - first).astype(dtype)
 
 
-def load_weights(step, order, parts, w_now, o_now):
-    width = w_now.shape[0] if w_now is not None else o_now.shape[1]
-    for index, part in enumerate(parts):
-
-        @pl.when(step == order(index))
-        def _(part=part):
-            cut = part.shape[1]
-            if w_now is not None:
-                for block in range(3):
-                    w_now[:, block * cut : (block + 1) * cut] = part[block * width : (block + 1) * width]
-            if o_now is not None:
-                for block in range(width // cut):
-                    begin = 3 * width + block * cut
-                    o_now[:, block * cut : (block + 1) * cut] = part[begin : begin + cut]
+def out_weights(part, width):
+    cut = part.shape[1]
+    base = part.shape[0] - width
+    blocks = [part[base + begin : base + begin + cut] for begin in range(0, width, cut)]
+    return jnp.concatenate(blocks, axis=1)
 
 
 def forward_kernel(pairs, chunk, chunks, *refs):
     place, lengths, tokens, gain_first = refs[:4]
     parts = refs[4 : 4 + pairs]
     gain_second = refs[4 + pairs]
-    normed, qkv_out, exps, inverse, attended, resid, second = refs[5 + pairs : 12 + pairs]
-    w_now, bias, attended_all = refs[12 + pairs :]
+    normed_out, qkv_out, exps, inverse, attended, resid, second = refs[5 + pairs : 12 + pairs]
+    normed, weights, bias, attended_all, arrived = refs[12 + pairs :]
     step = pl.program_id(0)
     width = tokens.shape[1]
     pair_width = attended.shape[2]
+    fetches = [
+        pltpu.make_async_copy(part, weights.at[index], arrived.at[index])
+        for index, part in enumerate(parts)
+    ]
     tiles = LONG // TILE
 
     @pl.when(step == 0)
     def _():
+        for fetch in fetches:
+            fetch.start()
         unit, _ = normalize(tokens[...].astype(F32))
         normed[...] = (unit * gain_first[...]).astype(BF)
         base = 4 * (place[1] * chunks + chunk)
@@ -132,8 +130,17 @@
             allowed = (col <= row) & (col >= begin)
             bias[pl.ds(row_tile * TILE, TILE), :] = jnp.where(allowed, 0.0, MASKED)
 
-    load_weights(step, lambda index: index, parts, w_now, None)
-    qkv = dot(normed[...], w_now[...]).astype(BF)
+    for index, fetch in enumerate(fetches):
+
+        @pl.when(step == index)
+        def _(fetch=fetch):
+            fetch.wait()
+
+    share = LONG // pairs
+    normed_out[...] = normed[pl.ds(pl.multiple_of(step * share, share), share), :]
+    own = weights[step, : 3 * width]
+    own = jnp.concatenate([own[begin : begin + width] for begin in range(0, 3 * width, width)], axis=1)
+    qkv = dot(normed[...], own).astype(BF)
     qkv_out[0] = qkv
     queries = qkv[:, :pair_width] * BF(HEAD_DIM**-0.5)
     key_rows = qkv[:, pair_width : 2 * pair_width]
@@ -160,7 +167,7 @@
             is_low, pltpu.roll(raw[0], HEAD_DIM, 1), pltpu.roll(raw[1], HEAD_DIM, 1)
         )
         inverted = 1.0 / totals
-        inverse[0, begin:extent] = inverted
+        inverse[0, begin:extent] = inverted.astype(BF)
         attended_tile = (jnp.where(is_low, raw[0], raw[1]) * inverted).astype(BF)
         attended[0, begin:extent] = attended_tile
         attended_all[step, begin:extent] = attended_tile
@@ -169,21 +176,9 @@
     def _():
         rows = jnp.concatenate([attended_all[index] for index in range(pairs)], axis=1)
         blocks = width // pair_width
-        weights = jnp.concatenate(
-            [
-                jnp.concatenate(
-                    [
-                        part[3 * width + block * pair_width : 3 * width + (block + 1) * pair_width]
-                        for block in range(blocks)
-                    ],
-                    axis=1,
-                )
-                for part in parts
-            ],
-            axis=0,
-        )
-        total = tokens[...].astype(F32) + dot(rows, weights)
-        resid[...] = total
+        own = jnp.concatenate([out_weights(weights[index], width) for index in range(pairs)], axis=0)
+        total = tokens[...].astype(F32) + dot(rows, own)
+        resid[...] = total.astype(BF)
         unit, _ = normalize(total)
         second[...] = (unit * gain_second[...]).astype(BF)
 
@@ -200,10 +195,10 @@
         f"forward_{chunk}",
         (pairs,),
         [scalars(), scalars(), pl.BlockSpec((LONG, width), lambda i: (chunk, 0)), whole(1, width)]
-        + [whole(packed, pair_width)] * pairs
+        + [pl.BlockSpec(memory_space=pl.ANY)] * pairs
         + [whole(1, width)],
         [
-            whole(LONG, width),
+            pl.BlockSpec((LONG // pairs, width), lambda i: (i, 0)),
             per_pair(LONG, triple),
             per_pair(2, kept, TILE, TILE),
             per_pair(LONG, pair_width),
@@ -215,39 +210,52 @@
             shape((LONG, width), BF),
             shape((pairs, LONG, triple), BF),
             shape((pairs, 2, kept, TILE, TILE), BF),
-            shape((pairs, LONG, pair_width), F32),
             shape((pairs, LONG, pair_width), BF),
-            shape((LONG, width), F32),
+            shape((pairs, LONG, pair_width), BF),
+            shape((LONG, width), BF),
             shape((LONG, width), BF),
         ],
         [
-            pltpu.VMEM((width, triple), BF),
+            pltpu.VMEM((LONG, width), BF),
+            pltpu.VMEM((pairs, packed, pair_width), BF),
             pltpu.VMEM((LONG, LONG), F32),
             pltpu.VMEM((pairs, LONG, pair_width), BF),
+            pltpu.SemaphoreType.DMA((pairs,)),
         ],
         (10e9, 25e6, 5e6),
+        limit=LARGE,
     )(place, lengths, tokens, gain_first, *parts, gain_second)
 
 
-def pack_kernel(slots, chunks, rows, out):
-    share = LONG // slots
+def pack_kernel(rows, out, arrived):
+    slots, chunks, share, _ = out.shape
+    copies = []
     for chunk in range(chunks):
         for index in range(slots):
             begin = chunk * LONG + index * share
-            out[index, chunk] = rows[begin : begin + share, :]
+            copies.append(
+                pltpu.make_async_copy(
+                    rows.at[pl.ds(begin, share)], out.at[index, chunk], arrived.at[len(copies)]
+                )
+            )
+    for copy in copies:
+        copy.start()
+    for copy in copies:
+        copy.wait()
 
 
 def pack_rows(rows, slots):
     total, width = rows.shape
     chunks, share = total // LONG, LONG // slots
     return call(
-        functools.partial(pack_kernel, slots, chunks),
+        pack_kernel,
         "pack_cotangent",
         (1,),
-        [whole(total, width)],
-        whole(slots, chunks, share, width),
+        [pl.BlockSpec(memory_space=pl.ANY)],
+        pl.BlockSpec(memory_space=pl.ANY),
         shape((slots, chunks, share, width), BF),
-        cost=(0, 4 * total * width, 0),
+        [pltpu.SemaphoreType.DMA((slots * chunks,))],
+        (0, 4 * total * width, 0),
     )(rows)
 
 
@@ -287,48 +295,36 @@
     grads = cotangents[...].reshape(LONG, width)
     logits = jnp.where(group_mask(slots, columns), dot(rows, control[...]), -1e30)
     powers = jnp.exp(logits - jnp.max(logits, axis=0, keepdims=True))
-    mixing = powers / jnp.sum(powers, axis=0, keepdims=True)
-    mixing_out[...] = mixing
-    low = mixing.astype(BF)
+    low = (powers / jnp.sum(powers, axis=0, keepdims=True)).astype(BF)
+    mixing_out[...] = low
     mixed = dot_rows(low, rows).astype(BF)
     grad_out = dot_rows(low, grads).astype(BF)
     for index in range(slots):
         part = slice(index * QUEUE, (index + 1) * QUEUE)
-        messages[index, 0, :QUEUE] = mixed[part]
-        messages[index, 0, QUEUE:] = grad_out[part]
+        messages[index, :QUEUE] = mixed[part]
+        messages[index, QUEUE:] = grad_out[part]
 
 
 def chunk_block(slots, rows, width, chunk):
     return pl.BlockSpec((slots, 1, rows, width), lambda i: (0, chunk, 0, 0))
 
 
-def mixing_part(chunk, control, members, cotangents, previous):
+def mixing_part(chunk, control, members, cotangents):
     slots, chunks, share, _ = cotangents.shape
     width, columns = control.shape
-    kernel = functools.partial(mixing_kernel, slots)
-    ins = [control, members, cotangents]
-    specs = [whole(width, columns), whole(LONG, width), chunk_block(slots, share, width, chunk)]
-    aliases = {}
-    if previous is not None:
-        aliases = {len(ins): 1}
-        kernel = without_previous(kernel, len(ins))
-        ins.append(previous)
-        specs.append(pl.BlockSpec(memory_space=pl.ANY))
-    return call(
-        kernel,
+    return call(
+        functools.partial(mixing_kernel, slots),
         f"mixing_{chunk}",
         (1,),
-        specs,
-        [whole(LONG, columns), chunk_block(slots, 2 * QUEUE, width, chunk)],
-        [shape((LONG, columns), F32), shape((slots, chunks, 2 * QUEUE, width), BF)],
-        (),
-        (6 * LONG * columns * width, 4e6, LONG * columns),
-        aliases,
-    )(*ins)
+        [whole(width, columns), whole(LONG, width), chunk_block(slots, share, width, chunk)],
+        [whole(LONG, columns), whole(slots, 2 * QUEUE, width)],
+        [shape((LONG, columns), BF), shape((slots, 2 * QUEUE, width), BF)],
+        cost=(6 * LONG * columns * width, 4e6, LONG * columns),
+    )(control, members, cotangents)
 
 
 def expert_kernel(slots, messages, w_expand, b_expand, w_reduce, b_reduce, *refs):
-    answers, taken, grads, activated_out, grad_pre_out, out_sum, mixed_sum = refs
+    answers, activated_out, grad_pre_out, taken, grads, out_sum, mixed_sum = refs
     step = pl.program_id(0)
 
     @pl.when(step == 0)
@@ -363,14 +359,14 @@
             answers[begin + QUEUE : begin + 2 * QUEUE] = mixed_sum[part].astype(BF)
 
 
-def expert_part(messages, w_expand, b_expand, w_reduce, b_reduce):
+def expert_part(chunk, messages, w_expand, b_expand, w_reduce, b_reduce):
     _, width, hidden = w_expand.shape
     count = messages.shape[0] // 2
     slots = count // QUEUE
     cut = min(512, hidden)
     outs = call(
         functools.partial(expert_kernel, slots),
-        "expert",
+        f"expert_{chunk}",
         (hidden // cut,),
         [
             whole(2 * count, width),
@@ -381,31 +377,31 @@
         ],
         [
             whole(2 * count, width),
-            whole(count, width),
-            whole(count, width),
             pl.BlockSpec((count, cut), lambda i: (0, i)),
             pl.BlockSpec((count, cut), lambda i: (0, i)),
         ],
-        [shape((2 * count, width), BF)]
-        + [shape((count, width), BF)] * 2
-        + [shape((count, hidden), BF)] * 2,
-        [pltpu.VMEM((count, width), F32), pltpu.VMEM((count, width), F32)],
+        [shape((2 * count, width), BF)] + [shape((count, hidden), BF)] * 2,
+        [pltpu.VMEM((count, width), BF)] * 2 + [pltpu.VMEM((count, width), F32)] * 2,
         (8 * count * width * hidden, 8e6, count * hidden),
     )(messages, w_expand, b_expand, w_reduce, b_reduce)
-    return outs[0], outs[1:]
+    return outs
 
 
 def expert_weights_kernel(chunks, place, *refs):
-    taken = refs[:chunks]
-    grads = refs[chunks : 2 * chunks]
-    activated = refs[2 * chunks : 3 * chunks]
-    grad_pre = refs[3 * chunks : 4 * chunks]
-    own, other, bias_e, bias_r, full_e, full_r = refs[4 * chunks :]
-    join = lambda parts: jnp.concatenate([part[...] for part in parts], axis=0)
-    pre = join(grad_pre)
-    cotangent = join(grads)
-    full_e[...] = dot_rows(join(taken), pre).astype(BF)
-    full_r[...] = dot_rows(join(activated), cotangent).astype(BF)
+    messages, activated, grad_pre = refs[:chunks], refs[chunks : 2 * chunks], refs[2 * chunks : 3 * chunks]
+    own, other, bias_e, bias_r, full_e, full_r = refs[3 * chunks :]
+    join = lambda parts: jnp.concatenate(parts, axis=0)
+    pick = lambda offset: join(
+        [
+            part[begin + offset : begin + offset + QUEUE]
+            for part in messages
+            for begin in range(0, part.shape[0], 2 * QUEUE)
+        ]
+    )
+    taken, cotangent = pick(0), pick(QUEUE)
+    pre = join([part[...] for part in grad_pre])
+    full_e[...] = dot_rows(taken, pre).astype(BF)
+    full_r[...] = dot_rows(join([part[...] for part in activated]), cotangent).astype(BF)
     bias_e[...] = jnp.sum(pre.astype(F32), axis=0, keepdims=True)
     bias_r[...] = jnp.sum(cotangent.astype(F32), axis=0, keepdims=True)
     begin = 0
@@ -416,25 +412,24 @@
         begin += cut
 
 
-def expert_weights(place, saved):
-    chunks = len(saved)
-    taken, grads, activated, grad_pre = zip(*saved)
-    count, width = taken[0].shape
-    hidden = activated[0].shape[1]
+def expert_weights(place, kept):
+    chunks = len(kept)
+    messages, activated, grad_pre = zip(*kept)
+    count, hidden = activated[0].shape
+    width = messages[0].shape[1]
     cut = width
-    steps = hidden // cut
     wide = lambda rows: pl.BlockSpec((rows, cut), lambda i: (0, i))
     tall = pl.BlockSpec((cut, width), lambda i: (i, 0))
     return call(
         functools.partial(expert_weights_kernel, chunks),
         "expert_weights",
-        (steps,),
-        [scalars()] + [whole(count, width)] * (2 * chunks) + [wide(count)] * (2 * chunks),
+        (hidden // cut,),
+        [scalars()] + [whole(2 * count, width)] * chunks + [wide(count)] * (2 * chunks),
         [tall, tall, wide(1), whole(1, width)],
         [shape((hidden, width), BF)] * 2 + [shape((1, hidden), F32), shape((1, width), F32)],
         [pltpu.VMEM((width, cut), BF), pltpu.VMEM((cut, width), BF)],
         (4 * chunks * count * width * hidden, 9e6, 0),
-    )(place, *taken, *grads, *activated, *grad_pre)
+    )(place, *messages, *activated, *grad_pre)
 
 
 def place_weights_kernel(place, own, own_across, other, other_across, out_e, out_r):
@@ -472,10 +467,10 @@
 def unmix_kernel(slots, control, mixing_ref, members, cotangents, answers, back, merged, control_out):
     rows = members[...]
     grads = cotangents[...].reshape(rows.shape)
-    pick = lambda part: jnp.concatenate([answers[index, 0, part] for index in range(slots)], axis=0)
+    pick = lambda part: jnp.concatenate([answers[index, part] for index in range(slots)], axis=0)
     expert_out, grad_mixed = pick(slice(0, QUEUE)), pick(slice(QUEUE, 2 * QUEUE))
-    mixing = mixing_ref[...]
-    low = mixing.astype(BF)
+    low = mixing_ref[...]
+    mixing = low.astype(F32)
     grad_mixing = dot_cols(grads, expert_out) + dot_cols(rows, grad_mixed)
     weighted = mixing * grad_mixing
     grad_logits = weighted - mixing * jnp.sum(weighted, axis=0, keepdims=True)
@@ -497,9 +492,8 @@
 
 
 def unmix_part(chunk, control, mixing, members, cotangents, answers, previous):
-    slots, chunks, _, width = answers.shape
+    slots, chunks, share, width = cotangents.shape
     columns = control.shape[1]
-    share = LONG // slots
     kernel = functools.partial(unmix_kernel, slots)
     ins = [control, mixing, members, cotangents, answers]
     specs = [
@@ -507,7 +501,7 @@
         whole(LONG, columns),
         whole(LONG, width),
         chunk_block(slots, share, width, chunk),
-        chunk_block(slots, 2 * QUEUE, width, chunk),
+        whole(slots, 2 * QUEUE, width),
     ]
     aliases = {}
     if previous is not None:
@@ -536,7 +530,7 @@
     merged, out = refs[chunks:]
     for chunk in range(chunks):
         rows = merged[:, chunk].reshape(LONG, out.shape[1]).astype(F32)
-        out[chunk * LONG : (chunk + 1) * LONG] = (refs[chunk][...] + rows).astype(BF)
+        out[chunk * LONG : (chunk + 1) * LONG] = (refs[chunk][...].astype(F32) + rows).astype(BF)
 
 
 def output_part(resids, merged):
@@ -552,7 +546,7 @@
     )(*resids, merged)
 
 
-def backward_kernel(pairs, begins, later, *refs):
+def backward_kernel(pairs, begins, later, split, *refs):
     refs = list(refs)
     take = lambda count: [refs.pop(0) for _ in range(count)]
     if begins:
@@ -561,35 +555,57 @@
         (resid_low,) = take(1)
     parts = take(len(pairs))
     normed, qkv, exps, inverse, attended = take(5)
-    weights_before = take(len(pairs)) if later else None
-    weights_out = take(len(pairs))
+    (weights_before,) = take(1) if later else (None,)
+    weights_out = take(len(pairs) if split else 1)
     (grads_out,) = take(1)
     if begins:
-        gains_out, grad_resid, resid_low = take(3)
-    normed_turned, w_now, o_now, queries_sum, keys_turned, values_turned = take(6)
+        gains_out, low_out = take(2)
+    normed_turned, o_now, grad_scores_all, exps_now, arrived = take(5)
+    if begins:
+        (resid_low,) = take(1)
     step = pl.program_id(0)
     pair_width = attended.shape[2]
     tiles = LONG // TILE
+
+    def fetch(index):
+        slot = lax.rem(index, 2)
+        return pltpu.make_async_copy(exps.at[pairs[0] - index], exps_now.at[slot], arrived.at[slot])
+
+    @pl.when(step == 0)
+    def _():
+        fetch(step).start()
+
+    @pl.when(step + 1 < len(pairs))
+    def _():
+        fetch(step + 1).start()
 
     @pl.when(step == 0)
     def _():
         normed_turned[...] = normed[...].T
         if begins:
-            unit, scaling = normalize(resid[...])
+            unit, scaling = normalize(resid[...].astype(F32))
             through, gain_grad = normalize_back(
                 back[...].astype(F32), gain_second[...], unit, scaling
             )
             gains_out[...] = gain_grad
-            total = grad_output[...].astype(F32) + through
-            grad_resid[...] = total
-            resid_low[...] = total.astype(BF)
-
-    load_weights(step, lambda index: index, parts, None, o_now)
+            resid_low[...] = (grad_output[...].astype(F32) + through).astype(BF)
+
+    for index, part in enumerate(parts):
+
+        @pl.when(step == index)
+        def _(part=part):
+            o_now[...] = out_weights(part[...], o_now.shape[1])
+
+    if begins:
+        share = low_out.shape[0]
+        low_out[...] = resid_low[pl.ds(pl.multiple_of(step * share, share), share), :]
     low = resid_low[...]
+    fetch(step).wait()
+    exps = exps_now.at[lax.rem(step, 2)]
     grad_attended = dot_cols(low, o_now[...]).astype(BF)
     grad_out_weights = dot_rows(attended[0], low)
     wide = grad_attended.astype(F32)
-    inverted = inverse[0]
+    inverted = inverse[0].astype(F32)
     scaled = wide * inverted
     products = scaled * attended[0].astype(F32)
     scaled = scaled.astype(BF)
@@ -599,27 +615,44 @@
     key_rows = qkv[0, :, pair_width : 2 * pair_width]
     value_rows = qkv[0, :, 2 * pair_width :]
     scaled_keys = key_rows * BF(HEAD_DIM**-0.5)
-    queries_sum[...] = jnp.zeros_like(queries_sum)
-    keys_turned[...] = jnp.zeros_like(keys_turned)
-    values_turned[...] = jnp.zeros_like(values_turned)
+    queries_turned = queries.T
+    grads_turned = scaled.T
+    ones = (high_half, low_half)
+    joined_q, joined_k, joined_v = [], [], []
     for head, (half, half_wide) in enumerate(((low_half, low_wide), (high_half, high_wide))):
         head_grads = scaled * half
-        head_queries = queries * half
         head_keys = scaled_keys * half
         deltas = jnp.sum(products * half_wide, axis=1, keepdims=True)
+        part = slice(head * HEAD_DIM, (head + 1) * HEAD_DIM)
+        query_rows = []
         for row_tile in range(tiles):
             begin, extent = row_tile * TILE, (row_tile + 1) * TILE
             powers = jnp.concatenate(
-                [exps[0, head, tile_slot(row_tile, col_tile)] for col_tile in range(row_tile + 1)],
+                [exps[head, tile_slot(row_tile, col_tile)] for col_tile in range(row_tile + 1)],
                 axis=1,
             )
             grad_probs = dot_cols(head_grads[begin:extent], value_rows[:extent])
             grad_scores = (powers.astype(F32) * (grad_probs - deltas[begin:extent])).astype(BF)
-            queries_sum[begin:extent] += dot(grad_scores, head_keys[:extent])
-            keys_turned[:, :extent] += dot_rows(head_queries[begin:extent], grad_scores)
-            values_turned[:, :extent] += dot_rows(head_grads[begin:extent], powers)
+            grad_scores_all[begin:extent, :extent] = grad_scores
+            query_rows.append(dot(grad_scores, head_keys[:extent]))
+        joined_q.append(jnp.concatenate(query_rows, axis=0))
+        key_cols, value_cols = [], []
+        for col_tile in range(tiles):
+            begin, extent = col_tile * TILE, (col_tile + 1) * TILE
+            powers = jnp.concatenate(
+                [exps[head, tile_slot(row_tile, col_tile)] for row_tile in range(col_tile, tiles)],
+                axis=0,
+            )
+            key_cols.append(dot(queries_turned[part, begin:], grad_scores_all[begin:, begin:extent]))
+            value_cols.append(dot(grads_turned[part, begin:], powers))
+        joined_k.append(jnp.concatenate(key_cols, axis=1))
+        joined_v.append(jnp.concatenate(value_cols, axis=1))
     grads = jnp.concatenate(
-        [queries_sum[...].astype(BF), keys_turned[...].T.astype(BF), values_turned[...].T.astype(BF)],
+        [
+            (joined_q[0] + joined_q[1]).astype(BF),
+            jnp.concatenate(joined_k, axis=0).T.astype(BF),
+            jnp.concatenate(joined_v, axis=0).T.astype(BF),
+        ],
         axis=1,
     )
     grads_out[0] = grads
@@ -630,20 +663,27 @@
         grad_out_weights[:, index * pair_width : (index + 1) * pair_width]
         for index in range(width // pair_width)
     ]
-    for index, out in enumerate(weights_out):
-
-        @pl.when(step == index)
-        def _(index=index, out=out):
-            begin = 0
-            for block in blocks:
-                extent = begin + block.shape[0]
-                if later:
-                    block = block + weights_before[index][begin:extent]
-                out[begin:extent] = block.astype(out.dtype)
-                begin = extent
-
-
-def backward_part(chunk, pairs, start, low, parts, saved, before, last):
+    def store(out):
+        begin = 0
+        for block in blocks:
+            extent = begin + block.shape[0]
+            if later:
+                block = block + weights_before[0, begin:extent].astype(F32)
+            out[begin:extent] = block.astype(BF)
+            begin = extent
+
+    if split:
+        for index, out in enumerate(weights_out):
+
+            @pl.when(step == index)
+            def _(out=out):
+                store(out)
+
+    else:
+        store(weights_out[0].at[0])
+
+
+def backward_part(chunk, pairs, start, low, parts, saved, before, split):
     exps = saved[2]
     width = saved[0].shape[1]
     packed, pair_width = parts[0].shape
@@ -659,26 +699,32 @@
     else:
         ins, specs = [low], [rows]
     ins += [parts[pair] for pair in pairs] + list(saved)
-    specs += [whole(packed, pair_width)] * len(pairs)
+    out_part = pl.BlockSpec((width, pair_width), lambda i: (packed // width - 1, 0))
+    specs += [out_part] * len(pairs)
     specs += [
         rows,
         per_pair(LONG, triple),
-        per_pair(2, kept, TILE, TILE),
+        pl.BlockSpec(memory_space=pl.ANY),
         per_pair(LONG, pair_width),
         per_pair(LONG, pair_width),
     ]
     if later:
-        ins += [before[pair] for pair in pairs]
-        specs += [whole(packed, pair_width)] * len(pairs)
-    out_specs = [whole(packed, pair_width)] * len(pairs)
-    outs = [shape((packed, pair_width), BF if last else F32)] * len(pairs)
+        ins.append(before)
+        specs.append(per_pair(packed, pair_width))
+    count = len(pairs) if split else 1
+    if split:
+        out_specs = [whole(packed, pair_width)] * count
+        outs = [shape((packed, pair_width), BF)] * count
+    else:
+        out_specs = [per_pair(packed, pair_width)]
+        outs = [shape((len(pairs), packed, pair_width), BF)]
     out_specs.append(pl.BlockSpec((1, LONG, triple), lambda i: (i, 0, 0)))
     outs.append(shape((len(pairs), LONG, triple), BF))
     if begins:
-        out_specs += [whole(1, width), rows, rows]
-        outs += [shape((1, width), F32), shape((LONG, width), F32), shape((LONG, width), BF)]
+        out_specs += [whole(1, width), pl.BlockSpec((LONG // len(pairs), width), lambda i: (i, 0))]
+        outs += [shape((1, width), F32), shape((LONG, width), BF)]
     results = call(
-        functools.partial(backward_kernel, pairs, begins, later),
+        functools.partial(backward_kernel, pairs, begins, later, split),
         f"backward_{chunk}_{first}",
         (len(pairs),),
         specs,
@@ -686,16 +732,17 @@
         outs,
         [
             pltpu.VMEM((width, LONG), BF),
-            pltpu.VMEM((width, triple), BF),
             pltpu.VMEM((pair_width, width), BF),
-            pltpu.VMEM((LONG, pair_width), F32),
-            pltpu.VMEM((pair_width, LONG), F32),
-            pltpu.VMEM((pair_width, LONG), F32),
-        ],
+            pltpu.VMEM((LONG, LONG), BF),
+            pltpu.VMEM((2, 2, kept, TILE, TILE), BF),
+            pltpu.SemaphoreType.DMA((2,)),
+        ]
+        + [pltpu.VMEM((LONG, width), BF)] * begins,
         (6e9 * len(pairs), 6e6 * len(pairs), 0),
+        limit=LARGE,
     )(*ins)
-    count = len(pairs)
-    return dict(zip(pairs, results[:count])), results[count], results[count + 1 :]
+    weights = dict(zip(pairs, results)) if split else results[0]
+    return weights, results[count], results[count + 1 :]
 
 
 def finish_kernel(groups, *refs):
@@ -734,7 +781,7 @@
                 dot_cols(joined, weights[...]), gain_first[...], unit, scaling
             )
             gain_out[...] += gain_grad
-            grad_tokens[...] = resids[chunk][...] + through
+            grad_tokens[...] = resids[chunk][...].astype(F32) + through
 
 
 def finish_part(tokens, gain_first, parts, groups, grads, resids):
@@ -755,6 +802,7 @@
         [shape((total, width), F32), shape((1, width), F32)],
         [pltpu.VMEM((width, 3 * pair_width * len(parts)), BF)],
         (2 * total * width * 3 * pair_width * len(parts), 2e7, 0),
+        limit=LARGE,
     )(tokens, gain_first, *parts, *flat, *resids)
 
 
@@ -778,33 +826,40 @@
     )(*parts)
 
 
-def tail_sum_kernel(slots, pieces, small, out):
+def tail_sum_kernel(slots, sent, pieces, *refs):
+    *parts, out, bias_e, bias_r = refs
+    small = tree_sum([part[...] for part in parts])
     share, cut = pieces.shape[1:]
     total = pieces[0].astype(F32)
     for index in range(1, slots):
         total = total + pieces[index].astype(F32)
     total = total.astype(BF)
     packed = jnp.concatenate(
-        [small[:, begin : begin + cut] for begin in range(0, small.shape[1], cut)], axis=0
+        [small[:sent, begin : begin + cut] for begin in range(0, small.shape[1], cut)], axis=0
     ).astype(BF)
     for index in range(slots):
         out[index, :share] = total
         out[index, share:] = packed
-
-
-def tail_sum(pieces, small):
+    width = bias_r.shape[1]
+    rows = bias_e.shape[1] // width
+    for index in range(rows):
+        bias_e[:, index * width : (index + 1) * width] = small[sent + index : sent + index + 1]
+    bias_r[...] = small[sent + rows : sent + rows + 1]
+
+
+def tail_sum(pieces, smalls, sent, hidden):
     slots, share, cut = pieces.shape
-    count, width = small.shape
-    rows = share + count * width // cut
-    return call(
-        functools.partial(tail_sum_kernel, slots),
+    count, width = smalls[0].shape
+    rows = share + sent * width // cut
+    return call(
+        functools.partial(tail_sum_kernel, slots, sent),
         "tail_sum",
         (1,),
-        [whole(slots, share, cut), whole(count, width)],
-        whole(slots, rows, cut),
-        shape((slots, rows, cut), BF),
+        [whole(slots, share, cut)] + [whole(count, width)] * len(smalls),
+        [whole(slots, rows, cut), whole(1, hidden), whole(1, width)],
+        [shape((slots, rows, cut), BF), shape((1, hidden), F32), shape((1, width), F32)],
         cost=(0, 2e6, 0),
-    )(pieces, small)
+    )(pieces, *smalls)
 
 
 def gather_kernel(slots, share, pieces, *refs):
@@ -828,15 +883,15 @@
     small = jnp.concatenate(
         [small[index * count : (index + 1) * count] for index in range(blocks)], axis=1
     )
-    experts = control.shape[1]
+    experts = control.shape[0]
     gain_first[...] = small[experts : experts + 1]
     gain_second[...] = small[experts + 1 : experts + 2]
-    control[...] = small[:experts].T
+    control[...] = small[:experts]
 
 
 def gather_weights(pieces, share, width, experts):
     slots, _, cut = pieces.shape
-    outs = [(width, cut)] * 3 + [(cut, width), (1, width), (1, width), (width, experts)]
+    outs = [(width, cut)] * 3 + [(cut, width), (1, width), (1, width), (experts, width)]
     return call(
         functools.partial(gather_kernel, slots, share),
         "gather_weights",
@@ -914,26 +969,25 @@
         forwards.append(saved)
         second = after(second, cotangents)
         members.append(exchange(second, "seq"))
-    mixings, messages = [], None
+    mixings, answers, kept = [], [], []
     for chunk in range(chunks):
-        mixing, messages = mixing_part(
-            chunk, control, members[chunk], cotangents, messages
-        )
+        mixing, messages = mixing_part(chunk, control, members[chunk], cotangents)
         mixings.append(mixing)
-    messages = exchange(messages, "seq")
-    replies, kept = expert_part(
-        messages.reshape(-1, width), w_expand, b_expand, w_reduce, b_reduce
-    )
-    answers = exchange(replies.reshape(messages.shape), "seq")
+        messages = exchange(messages, "seq")
+        flat = messages.reshape(-1, width)
+        replies, *saved = expert_part(chunk, flat, w_expand, b_expand, w_reduce, b_reduce)
+        kept.append((flat, *saved))
+        answers.append(exchange(replies.reshape(messages.shape), "seq"))
     backs, merged, controls = [], None, []
     for chunk in range(chunks):
         back, merged, grad_control = unmix_part(
-            chunk, control, mixings[chunk], members[chunk], cotangents, answers, merged
+            chunk, control, mixings[chunk], members[chunk], cotangents, answers[chunk], merged
         )
+        early_back = back if chunk == 0 else early_back
         backs.append(exchange(back, "seq"))
         controls.append(grad_control)
 
-    own, other, bias_e, bias_r = expert_weights(place, [kept])
+    own, other, bias_e, bias_r = expert_weights(place, [after(kept[0], early_back), *kept[1:]])
     own = add_low(own, partner(other, "head", 1))
     across = partner(own, "head", 2)
     placed = (own, across, partner(own, "head", 1), partner(across, "head", 1))
@@ -950,45 +1004,45 @@
             merged = exchange(merged, "seq")
             back = after(back, across)
             start = (back, resid, grad_output, gain_second)
-            first_weights, first_grads, (gain, grad_resid, low) = backward_part(
+            first_weights, first_grads, (gain, low) = backward_part(
                 chunk, early, start, None, parts, saved, before, True
             )
-            pieces = [partner(first_weights[pair], "head", pair) for pair in early]
+            joint = add_low(first_weights[2], partner(first_weights[3], "head", 1))
+            pieces = [partner(joint, "head", 2)]
             second_weights, second_grads, _ = backward_part(
-                chunk, late, None, low, parts, saved, before, True
+                chunk, late, None, after(low, joint), parts, saved, before, True
             )
             groups.append((early, late))
             grads.append((first_grads, second_grads))
         else:
             start = (back, resid, grad_output, gain_second)
-            before, chunk_grads, (gain, grad_resid, low) = backward_part(
+            before, chunk_grads, (gain, low) = backward_part(
                 chunk, pairs, start, None, parts, saved, before, False
             )
             groups.append((pairs,))
             grads.append((chunk_grads,))
         gains.append(gain)
-        resids.append(grad_resid)
+        resids.append(low)
     resids[-1] = after(resids[-1], *pieces)
     grad_tokens, gain = finish_part(tokens, gain_first, parts, groups, grads, resids)
 
-    pieces += [partner(second_weights[pair], "head", pair) for pair in late if pair]
+    pieces.append(partner(after(second_weights[1], *pieces), "head", 1))
     packed = tail_pack([second_weights[0]] + pieces)
-    packed = after(packed, merged, *placed)
+    hidden = bias_e.shape[1]
+    sent = -(-(experts + 2) // 8) * 8
+    spare = jnp.zeros((sent - experts - 2, width), F32)
+    small = [sum(controls), gain, sum(gains), spare, bias_e.reshape(-1, width), bias_r]
+    small = jnp.concatenate(small, axis=0)
+    smalls = [small] + [partner(small, "head", index) for index in range(1, len(parts))]
+    packed = after(packed, merged, *smalls, *placed)
     pieces = exchange(packed, "seq").reshape(slots, -1, pair_width)
-
-    hidden_rows = bias_e.shape[1] // width
-    small = [sum(controls), gain, sum(gains), bias_e.reshape(-1, width), bias_r]
-    used = experts + 3 + hidden_rows
-    small = jnp.concatenate(small + [jnp.zeros((-used % 8, width), F32)], axis=0)
-    small = tree_sum([small] + [partner(small, "head", index) for index in range(1, len(parts))])
-    sent = -(-(experts + 2) // 8) * 8
-    pieces = exchange(tail_sum(pieces, small[:sent]), "seq")
+    pieces, grad_expand_bias, grad_reduce_bias = tail_sum(pieces, smalls, sent, hidden)
+    pieces = exchange(pieces, "seq")
     share = parts[0].shape[0] // slots
     *weights, gain_first, gain_second, control = gather_weights(pieces, share, width, experts)
     grad_query, grad_key, grad_value, grad_w_out = weights
     grad_expand, grad_reduce = place_weights(place, *placed)
     output = output_part([saved[5] for saved in forwards], merged)
-    after_gains = experts + 2
     return (
         output,
         grad_tokens,
@@ -998,11 +1052,11 @@
         grad_value,
         grad_w_out,
         gain_second[0],
-        control,
+        control.T,
         grad_expand,
-        small[after_gains : after_gains + hidden_rows].reshape(1, -1),
+        grad_expand_bias,
         grad_reduce,
-        small[after_gains + hidden_rows : used],
+        grad_reduce_bias,
     )
 
 

time: 391 us -> 363 us (0.928)
  Pallas kernels: 176 us -> 149 us
  local copies, waits for them, and re-layouts: 12.6 us -> 26.6 us
  waiting for transfers between devices: 106 us -> 95.8 us
  blocking collectives: 29.7 us -> 21 us
    ppermute x13, waiting for transfers between devices: 39.4 us -> 14.7 us  [partner(): lax.ppermute(value, axis, [(index, index ^ offset) for index in range(cou...]
    unnamed x41 -> x100, local copies, waits for them, and re-layouts: 9.21 us -> 25.2 us
    all_to_all x9 -> x11, waiting for transfers between devices: 67 us -> 81.1 us  [exchange(): return lax.all_to_all(value, axis, 0, 0, tiled=True)]
    pallas_call x8 -> x9, Pallas kernels: 81 us -> 68.8 us  [the longest x3 47.9 us: backward_part(): call(functools.partial(backward_kernel, pairs, begins, later, split), f'b...]
    all_to_all x1, blocking collectives: 29.7 us -> 21 us  [exchange(): return lax.all_to_all(value, axis, 0, 0, tiled=True)]
    all_to_all x9 -> x11, starting transfers between devices: 44.6 us -> 48.2 us  [exchange(): return lax.all_to_all(value, axis, 0, 0, tiled=True)]
  transfers between devices with their start and end apart: 22 -> 24, of which waited for: 12 -> 12; matrix products, arithmetic and copies ran while one was open for 3% -> 2% of each run, Pallas kernels for 40% -> 41%
where the time goes in v1:
time: 363 us; the launch traced here: 356 us
  Pallas kernels  149 us (41%)
  waiting for transfers between devices  95.8 us (26%)
  starting transfers between devices  55.7 us (15%)
  local copies, waits for them, and re-layouts  26.6 us (7%)
  blocking collectives  21 us (6%)
  other arithmetic  7.2 us (2%)
    all_to_all x11, waiting for transfers between devices, exchange(): return lax.all_to_all(value, axis, 0, 0, tiled=True)  81.1 us
    all_to_all x11, starting transfers between devices, exchange(): return lax.all_to_all(value, axis, 0, 0, tiled=True)  48.2 us
    pallas_call x3, Pallas kernels, backward_part(): call(functools.partial(backward_kernel, pairs, begins, later, split), f'b...  47.9 us
    pallas_call x2, Pallas kernels, forward_part(): call(functools.partial(forward_kernel, pairs, chunk, rows // LONG), f'for...  43 us
    unnamed x100, local copies, waits for them, and re-layouts  25.2 us
    all_to_all x1, blocking collectives, exchange(): return lax.all_to_all(value, axis, 0, 0, tiled=True)  21 us
    ppermute x13, waiting for transfers between devices, partner(): lax.ppermute(value, axis, [(index, index ^ offset) for index in range(cou...  14.7 us
    pallas_call x1, Pallas kernels, finish_part(): call(functools.partial(finish_kernel, groups), 'finish', (chunks,), [rows...  11.3 us
  transfers between devices with their start and end apart: 24, of which 12 were waited for; matrix products, arithmetic and copies ran while one was open for 2% of the time, Pallas kernels for 41%

profile of v1, /device:TPU:0, one launch (start us, length us, event | category | flops | bytes accessed | tf_op | source)
XLA Modules:
  0.0 356.4 jit_solution(11925080068973344334)
XLA Ops:
  0.7 1.6 copy-done.5
  2.2 1.4 pack_cotangent.1
  3.7 7.4 %all-to-all-start = ((bf16[8,2,128,512]{3,2,1,0:T(8,128)(2,1)}), bf16[8,2,128,512]{3,2,1,0:T(8,128)(2,1)}, u32[]{:S(2)}, u32[]{:S(2)}) async-start(bf16[8,2,128,512]{3,2,1,0:T(8,128)(2,1)} %pack_cotangent.1), calls=%async_computation | async-start | bytes 4194304 | tf_op jit(solution)/shard_map/all_to_all | solution.py:913
  11.3 1.6 collective-permute-start.1
  12.8 11.9 %collective-permute-done.1.refs_6_.refs_5_.refs_4_ = bf16[2048,128]{1,0:T(8,128)(2,1)S(1)} collective-permute-done((bf16[2048,128]{1,0:T(8,128)(2,1)S(1)}, bf16[2048,128]{1,0:T(8,128)(2,1)S(1)}, u32[]{:S(2)}, u32[]{:S(2)}) %collective-permute-start.1) | collective-permute-done | bytes 524320 | tf_op jit(solution)/shard_map/ppermute | solution.py:909
  25.4 1.2 collective-permute-done.2.refs_7_.refs_4_.refs_5_
  27.4 21.5 %forward_0.1 = (bf16[1024,512]{1,0:T(8,128)(2,1)}, bf16[4,1024,384]{2,1,0:T(8,128)(2,1)}, bf16[4,2,10,256,256]{4,3,2,1,0:T(8,128)(2,1)}, bf16[4,1024,128]{2,1,0:...) custom-call(s32[2]{0:T(128)} %pad_add_fusion.refs_0_.place, ...), custom_call_target="tpu_custom_call" | custom-call | flops 10000000000 | bytes 25000000 | tf_op jit(solution)/shard_map/forward_0/pallas_call | solution.py:193
  48.9 10.6 %all-to-all-done.cotangents.refs_3_ = bf16[8,2,128,512]{3,2,1,0:T(8,128)(2,1)} async-done(((bf16[8,2,128,512]{3,2,1,0:T(8,128)(2,1)}), bf16[8,2,128,512]{3,2,1,0:T(8,128)(2,1)}, u32[]{:S(2)}, u32[]{:S(2)}) %all-to-all-start) | async-done | bytes 2097184 | tf_op jit(solution)/shard_map/all_to_all | solution.py:913
  59.5 3.8 %all-to-all-start.4 = ((bf16[8,128,512]{2,1,0:T(8,128)(2,1)}), bf16[8,128,512]{2,1,0:T(8,128)(2,1)S(1)}, u32[]{:S(2)}, u32[]{:S(2)}) async-start(bf16[8,128,512]{2,1,0:T(8,128)(2,1)} %bitcast.33), calls=%async_computation.4 | async-start | bytes 2097152 | tf_op jit(solution)/shard_map/all_to_all | solution.py:913
  63.3 21.5 %forward_1.1 = (bf16[1024,512]{1,0:T(8,128)(2,1)}, bf16[4,1024,384]{2,1,0:T(8,128)(2,1)}, bf16[4,2,10,256,256]{4,3,2,1,0:T(8,128)(2,1)}, bf16[4,1024,128]{2,1,0:...) custom-call(s32[2]{0:T(128)} %pad_add_fusion.refs_0_.place, ...), custom_call_target="tpu_custom_call" | custom-call | flops 10000000000 | bytes 25000000 | tf_op jit(solution)/shard_map/forward_1/pallas_call | solution.py:193
  84.9 4.4 %all-to-all-done.4 = bf16[8,128,512]{2,1,0:T(8,128)(2,1)S(1)} async-done(((bf16[8,128,512]{2,1,0:T(8,128)(2,1)}), bf16[8,128,512]{2,1,0:T(8,128)(2,1)S(1)}, u32[]{:S(2)}, u32[]{:S(2)}) %all-to-all-start.4) | async-done | bytes 1048608 | tf_op jit(solution)/shard_map/all_to_all | solution.py:913
  89.2 3.6 %all-to-all-start.1 = ((bf16[8,128,512]{2,1,0:T(8,128)(2,1)}), bf16[8,128,512]{2,1,0:T(8,128)(2,1)S(1)}, u32[]{:S(2)}, u32[]{:S(2)}) async-start(bf16[8,128,512]{2,1,0:T(8,128)(2,1)} %bitcast.34), calls=%async_computation.1 | async-start | bytes 2097152 | tf_op jit(solution)/shard_map/all_to_all | solution.py:913
  93.1 4.0 %mixing_0.1 = (bf16[1024,256]{1,0:T(8,128)(2,1)S(1)}, bf16[8,64,512]{2,1,0:T(8,128)(2,1)}) custom-call(bf16[512,256]{1,0:T(8,128)(2,1)S(1)} %copy.32.control.refs_0_, bf16[1024,512]{1,0:T(8,128)(2,1)S(1)} %bitcast.23, bf16[8,2,128,512]{3,2,1,0:T(8,128)(2,1)} %all-to-all-done.cotangents.refs_3_), custom_call_target="tpu_custom_call" | custom-call | flops 805306368 | bytes 4000000 | tf_op jit(solution)/shard_map/mixing_0/pallas_call | solution.py:315
  97.9 20.9 %all-to-all-done.1 = bf16[8,128,512]{2,1,0:T(8,128)(2,1)S(1)} async-done(((bf16[8,128,512]{2,1,0:T(8,128)(2,1)}), bf16[8,128,512]{2,1,0:T(8,128)(2,1)S(1)}, u32[]{:S(2)}, u32[]{:S(2)}) %all-to-all-start.1) | async-done | bytes 1048608 | tf_op jit(solution)/shard_map/all_to_all | solution.py:913
  118.8 3.6 %all-to-all-start.5 = ((bf16[8,64,512]{2,1,0:T(8,128)(2,1)}), bf16[8,64,512]{2,1,0:T(8,128)(2,1)S(1)}, u32[]{:S(2)}, u32[]{:S(2)}) async-start(bf16[8,64,512]{2,1,0:T(8,128)(2,1)} %get-tuple-element.94), calls=%async_computation.5 | async-start | bytes 1048576 | tf_op jit(solution)/shard_map/all_to_all | solution.py:913
  122.5 4.0 %mixing_1.1 = (bf16[1024,256]{1,0:T(8,128)(2,1)S(1)}, bf16[8,64,512]{2,1,0:T(8,128)(2,1)}) custom-call(bf16[512,256]{1,0:T(8,128)(2,1)S(1)} %copy.32.control.refs_0_, bf16[1024,512]{1,0:T(8,128)(2,1)S(1)} %bitcast.21, bf16[8,2,128,512]{3,2,1,0:T(8,128)(2,1)} %all-to-all-done.cotangents.refs_3_), custom_call_target="tpu_custom_call" | custom-call | flops 805306368 | bytes 4000000 | tf_op jit(solution)/shard_map/mixing_1/pallas_call | solution.py:315
  127.3 9.8 %all-to-all-done.5 = bf16[8,64,512]{2,1,0:T(8,128)(2,1)S(1)} async-done(((bf16[8,64,512]{2,1,0:T(8,128)(2,1)}), bf16[8,64,512]{2,1,0:T(8,128)(2,1)S(1)}, u32[]{:S(2)}, u32[]{:S(2)}) %all-to-all-start.5) | async-done | bytes 524320 | tf_op jit(solution)/shard_map/all_to_all | solution.py:913
  137.1 3.6 %all-to-all-start.2 = ((bf16[8,64,512]{2,1,0:T(8,128)(2,1)}), bf16[8,64,512]{2,1,0:T(8,128)(2,1)S(1)}, u32[]{:S(2)}, u32[]{:S(2)}) async-start(bf16[8,64,512]{2,1,0:T(8,128)(2,1)} %get-tuple-element.89), calls=%async_computation.2 | async-start | bytes 1048576 | tf_op jit(solution)/shard_map/all_to_all | solution.py:913
  140.8 1.6 copy-done.27
  142.4 1.6 copy-done.29
  144.0 5.2 %expert_0.1 = (bf16[512,512]{1,0:T(8,128)(2,1)}, bf16[256,2048]{1,0:T(8,128)(2,1)S(1)}, bf16[256,2048]{1,0:T(8,128)(2,1)S(1)}) custom-call(bf16[512,512]{1,0:T(8,128)(2,1)S(1)} %bitcast.28, bf16[1,512,2048]{2,1,0:T(8,128)(2,1)S(1)} %copy-done.27, f32[1,2048]{1,0:T(1,128)S(1)} %copy-done.33, bf16[1,2048,512]{2,1,0:T(8,128)(2,1)S(1)} %copy-done.29, ...), custom_call_target="tpu_custom_call" | custom-call | flops 2147483648 | bytes 8000000 | tf_op jit(solution)/shard_map/expert_0/pallas_call | solution.py:367
  150.2 1.1 copy-done.37
  151.3 4.2 %all-to-all-done.2 = bf16[8,64,512]{2,1,0:T(8,128)(2,1)S(1)} async-done(((bf16[8,64,512]{2,1,0:T(8,128)(2,1)}), bf16[8,64,512]{2,1,0:T(8,128)(2,1)S(1)}, u32[]{:S(2)}, u32[]{:S(2)}) %all-to-all-start.2) | async-done | bytes 524320 | tf_op jit(solution)/shard_map/all_to_all | solution.py:913
  155.5 3.6 %all-to-all-start.6 = ((bf16[8,64,512]{2,1,0:T(8,128)(2,1)}), bf16[8,64,512]{2,1,0:T(8,128)(2,1)S(1)}, u32[]{:S(2)}, u32[]{:S(2)}) async-start(bf16[8,64,512]{2,1,0:T(8,128)(2,1)} %bitcast.12), calls=%async_computation.6 | async-start | bytes 1048576 | tf_op jit(solution)/shard_map/all_to_all | solution.py:913
  159.1 1.6 copy-done.28
  160.7 1.6 copy-done.30
  162.3 5.2 %expert_1.1 = (bf16[512,512]{1,0:T(8,128)(2,1)}, bf16[256,2048]{1,0:T(8,128)(2,1)S(1)}, bf16[256,2048]{1,0:T(8,128)(2,1)S(1)}) custom-call(bf16[512,512]{1,0:T(8,128)(2,1)S(1)} %bitcast.30, bf16[1,512,2048]{2,1,0:T(8,128)(2,1)S(1)} %copy-done.28, f32[1,2048]{1,0:T(1,128)S(1)} %copy-done.33, bf16[1,2048,512]{2,1,0:T(8,128)(2,1)S(1)} %copy-done.30, ...), custom_call_target="tpu_custom_call" | custom-call | flops 2147483648 | bytes 8000000 | tf_op jit(solution)/shard_map/expert_1/pallas_call | solution.py:367
  167.5 1.0 copy-done.39
  168.5 1.0 copy-done.41
  169.5 4.2 %all-to-all-done.6.answers = bf16[8,64,512]{2,1,0:T(8,128)(2,1)S(1)} async-done(((bf16[8,64,512]{2,1,0:T(8,128)(2,1)}), bf16[8,64,512]{2,1,0:T(8,128)(2,1)S(1)}, u32[]{:S(2)}, u32[]{:S(2)}) %all-to-all-start.6) | async-done | bytes 524320 | tf_op jit(solution)/shard_map/all_to_all | solution.py:913
  173.8 4.4 %all-to-all-start.3 = ((bf16[8,64,512]{2,1,0:T(8,128)(2,1)}), bf16[8,64,512]{2,1,0:T(8,128)(2,1)}, u32[]{:S(2)}, u32[]{:S(2)}) async-start(bf16[8,64,512]{2,1,0:T(8,128)(2,1)} %bitcast.8), calls=%async_computation.3 | async-start | bytes 1048576 | tf_op jit(solution)/shard_map/all_to_all | solution.py:913
  178.2 1.2 copy-done.2
  179.4 1.0 copy-done.18
  180.4 1.0 copy-done.32
  181.5 4.4 %unmix_0.1 = (bf16[1024,512]{1,0:T(8,128)(2,1)S(1)}, bf16[8,2,128,512]{3,2,1,0:T(8,128)(2,1)S(1)}, f32[8,512]{1,0:T(8,128)S(1)}) custom-call(bf16[512,256]{1,0:T(8,128)(2,1)S(1)} %copy.32.control.refs_0_, bf16[1024,256]{1,0:T(8,128)(2,1)S(1)} %copy-done.32, bf16[1024,512]{1,0:T(8,128)(2,1)S(1)} %bitcast.24, ...), custom_call_target="tpu_custom_call" | custom-call | flops 1610612736 | bytes 6000000 | tf_op jit(solution)/shard_map/unmix_0/pallas_call | solution.py:512
  185.9 1.0 copy-done.7
  187.0 5.1 %expert_weights.1 = (bf16[2048,512]{1,0:T(8,128)(2,1)S(1)}, bf16[2048,512]{1,0:T(8,128)(2,1)}, f32[1,2048]{1,0:T(1,128)S(1)}, f32[1,512]{1,0:T(1,128)S(1)}) custom-call(s32[2]{0:T(128)S(1)} %copy-done.26, bf16[512,512]{1,0:T(8,128)(2,1)S(1)} %bitcast.29, bf16[512,512]{1,0:T(8,128)(2,1)S(1)} %bitcast.31, bf16[256,2048]{1,0:T(8,128)(2,1)S(1)} %copy-done.36, ...), custom_call_target="tpu_custom_call" | custom-call | flops 2147483648 | bytes 9000000 | tf_op jit(solution)/shard_map/expert_weights/pallas_call | solution.py:423
  192.1 1.4 copy-done.3
  193.5 6.0 %all-to-all-start.7 = ((bf16[8,128,512]{2,1,0:T(8,128)(2,1)}), bf16[8,128,512]{2,1,0:T(8,128)(2,1)}, u32[]{:S(2)}, u32[]{:S(2)}) async-start(bf16[8,128,512]{2,1,0:T(8,128)(2,1)} %bitcast.26), calls=%async_computation.7 | async-start | bytes 2097152 | tf_op jit(solution)/shard_map/all_to_all | solution.py:913
  199.5 1.0 copy-done.12
  200.5 4.5 %unmix_1.1 = (bf16[1024,512]{1,0:T(8,128)(2,1)S(1)}, bf16[8,2,128,512]{3,2,1,0:T(8,128)(2,1)S(1)}, f32[8,512]{1,0:T(8,128)S(1)}) custom-call(bf16[512,256]{1,0:T(8,128)(2,1)S(1)} %copy.32.control.refs_0_, bf16[1024,256]{1,0:T(8,128)(2,1)S(1)} %copy-done.12, bf16[1024,512]{1,0:T(8,128)(2,1)S(1)} %bitcast.22, ...), custom_call_target="tpu_custom_call", output_to_operand_aliasing={{1}: (5, {})} | custom-call | flops 1610612736 | bytes 6000000 | tf_op jit(solution)/shard_map/unmix_1/pallas_call | solution.py:512
  205.1 4.7 %add_convert_fusion.own = bf16[2048,512]{1,0:T(8,128)(2,1)} fusion(bf16[2048,512]{1,0:T(8,128)(2,1)} %collective-permute-done.3, bf16[2048,512]{1,0:T(8,128)(2,1)S(1)} %copy-done.4), kind=kLoop, calls=%fused_computation | loop fusion | flops 4194304 | bytes 6291456 | tf_op jit(solution)/shard_map/convert_element_type | solution.py:929
  209.8 1.5 collective-permute-start.4
  211.3 14.7 %all-to-all-done.7 = bf16[8,128,512]{2,1,0:T(8,128)(2,1)} async-done(((bf16[8,128,512]{2,1,0:T(8,128)(2,1)}), bf16[8,128,512]{2,1,0:T(8,128)(2,1)}, u32[]{:S(2)}, u32[]{:S(2)}) %all-to-all-start.7) | async-done | bytes 1048608 | tf_op jit(solution)/shard_map/all_to_all | solution.py:913
  226.0 3.6 %all-to-all-start.9 = ((bf16[8,128,512]{2,1,0:T(8,128)(2,1)}), bf16[8,128,512]{2,1,0:T(8,128)(2,1)S(1)}, u32[]{:S(2)}, u32[]{:S(2)}) async-start(bf16[8,128,512]{2,1,0:T(8,128)(2,1)} %bitcast.27), calls=%async_computation.9 | async-start | bytes 2097152 | tf_op jit(solution)/shard_map/all_to_all | solution.py:913
  229.6 20.8 %backward_0_3.1 = (bf16[4,2048,128]{2,1,0:T(8,128)(2,1)}, bf16[4,1024,384]{2,1,0:T(8,128)(2,1)}, f32[1,512]{1,0:T(1,128)}, bf16[1024,512]{1,0:T(8,128)(2,1)}) custom-call(bf16[1024,512]{1,0:T(8,128)(2,1)} %bitcast.14.refs_0_, bf16[1024,512]{1,0:T(8,128)(2,1)} %get-tuple-element.84.refs_1_.refs_0_, bf16[2048,512]{1,0:T(8,128)(2,1)} %refs_2_.7, ...), custom_call_target="tpu_custom_call" | custom-call | flops 24000000000 | bytes 24000000 | tf_op jit(solution)/shard_map/backward_0_3/pallas_call | solution.py:726
  250.5 5.2 %all-to-all-done.9 = bf16[8,128,512]{2,1,0:T(8,128)(2,1)S(1)} async-done(((bf16[8,128,512]{2,1,0:T(8,128)(2,1)}), bf16[8,128,512]{2,1,0:T(8,128)(2,1)S(1)}, u32[]{:S(2)}, u32[]{:S(2)}) %all-to-all-start.9) | async-done | bytes 1048608 | tf_op jit(solution)/shard_map/all_to_all | solution.py:913
  256.6 4.8 %all-to-all-start.8 = ((bf16[8,2,128,512]{3,2,1,0:T(8,128)(2,1)}), bf16[8,2,128,512]{3,2,1,0:T(8,128)(2,1)}, u32[]{:S(2)}, u32[]{:S(2)}) async-start(bf16[8,2,128,512]{3,2,1,0:T(8,128)(2,1)} %copy-done), calls=%async_computation.8 | async-start | bytes 4194304 | tf_op jit(solution)/shard_map/all_to_all | solution.py:913
  261.4 14.1 %backward_1_3.1 = (bf16[2048,128]{1,0:T(8,128)(2,1)}, bf16[2048,128]{1,0:T(8,128)(2,1)}, bf16[2,1024,384]{2,1,0:T(8,128)(2,1)}, f32[1,512]{1,0:T(1,128)}, bf16[1024,512]{1,0:T(8,128)(2,1)}) custom-call(bf16[1024,512]{1,0:T(8,128)(2,1)} %bitcast.32, bf16[1024,512]{1,0:T(8,128)(2,1)} %get-tuple-element.85.refs_1_, bf16[2048,512]{1,0:T(8,128)(2,1)} %refs_2_.7, ...), custom_call_target="tpu_custom_call" | custom-call | flops 12000000000 | bytes 12000000 | tf_op jit(solution)/shard_map/backward_1_3/pallas_call | solution.py:726
  276.1 1.5 collective-permute-done.5
  277.6 1.2 add_convert_fusion.1
  278.8 1.6 collective-permute-start.6
  280.4 13.0 %backward_1_1.1 = (bf16[2048,128]{1,0:T(8,128)(2,1)}, bf16[2048,128]{1,0:T(8,128)(2,1)}, bf16[2,1024,384]{2,1,0:T(8,128)(2,1)}) custom-call(bf16[1024,512]{1,0:T(8,128)(2,1)} %get-tuple-element.131.refs_0_.refs_10_, bf16[2048,128]{1,0:T(8,128)(2,1)} %copy-done.45, bf16[2048,128]{1,0:T(8,128)(2,1)} %copy-done.6, ...), custom_call_target="tpu_custom_call" | custom-call | flops 12000000000 | bytes 12000000 | tf_op jit(solution)/shard_map/backward_1_1/pallas_call | solution.py:726
  294.7 11.3 %finish.1 = (f32[2048,512]{1,0:T(8,128)}, f32[1,512]{1,0:T(1,128)}) custom-call(bf16[2048,512]{1,0:T(8,128)(2,1)} %refs_0_.1, f32[1,512]{1,0:T(1,128)} %bitcast.38, bf16[2048,128]{1,0:T(8,128)(2,1)} %copy-done.6, bf16[2048,128]{1,0:T(8,128)(2,1)} %copy-done.45, bf16[2048,128]{1,0:T(8,128)(2,1)} %copy-done.44, bf16[2048,128]{1,0:T(8,128)(2,1)} %copy-done.46, ...), custom_call_target="tpu_custom_call" | custom-call | flops 3221225472 | bytes 20000000 | tf_op jit(solution)/shard_map/finish/pallas_call | solution.py:793
  306.8 1.0 collective-permute-start.10
  307.8 1.2 collective-permute-start.9
  309.8 1.0 copy-done.19
  310.8 1.0 copy-done.21
  312.1 21.0 %all_to_all.89.pieces = bf16[8,256,128]{2,1,0:T(8,128)(2,1)S(1)} all-to-all(bf16[8,256,128]{2,1,0:T(8,128)(2,1)S(1)} %bitcast.25), channel_id=1, replica_groups=mesh['seq'=8,'head'=4] {'seq'}, dimensions={0} | all-to-all | bytes 1048576 | tf_op jit(solution)/shard_map/all_to_all | solution.py:913
  334.1 3.6 %all-to-all-start.11 = ((bf16[8,320,128]{2,1,0:T(8,128)(2,1)}), bf16[8,320,128]{2,1,0:T(8,128)(2,1)S(1)}, u32[]{:S(2)}, u32[]{:S(2)}) async-start(bf16[8,320,128]{2,1,0:T(8,128)(2,1)} %get-tuple-element.143), calls=%async_computation.11 | async-start | bytes 1310720 | tf_op jit(solution)/shard_map/all_to_all | solution.py:913
  337.8 3.4 output.1
  341.1 7.0 %place_expert_weights.1 = (f32[1,512,2048]{2,1,0:T(8,128)}, f32[1,2048,512]{2,1,0:T(8,128)}) custom-call(s32[2]{0:T(128)S(1)} %copy-done.26, bf16[2048,512]{1,0:T(8,128)(2,1)} %add_convert_fusion.own, bf16[2048,512]{1,0:T(8,128)(2,1)} %collective-permute-done.4.own_across, bf16[2048,512]{1,0:T(8,128)(2,1)} %collective-permute-done.11.other, ...), custom_call_target="tpu_custom_call" | custom-call | bytes 16777216 | tf_op jit(solution)/shard_map/place_expert_weights/pallas_call | solution.py:453
  348.1 7.1 %all-to-all-done.11.pieces = bf16[8,320,128]{2,1,0:T(8,128)(2,1)S(1)} async-done(((bf16[8,320,128]{2,1,0:T(8,128)(2,1)}), bf16[8,320,128]{2,1,0:T(8,128)(2,1)S(1)}, u32[]{:S(2)}, u32[]{:S(2)}) %all-to-all-start.11) | async-done | bytes 655392 | tf_op jit(solution)/shard_map/all_to_all | solution.py:913
  355.2 1.0 gather_weights.1
  (117 shorter events, 10.0 us)
Async XLA Ops:
  0.6 1.6 copy-start.5
  3.7 7.5 %copy-start.22 = (bf16[512,128]{1,0:T(8,128)(2,1)S(1)}, bf16[512,128]{1,0:T(8,128)(2,1)}, u32[]{:S(2)}) copy-start(bf16[512,128]{1,0:T(8,128)(2,1)} %query.1) | copy-start | bytes 393220
  3.7 7.5 %copy-start.23 = (bf16[512,128]{1,0:T(8,128)(2,1)S(1)}, bf16[512,128]{1,0:T(8,128)(2,1)}, u32[]{:S(2)}) copy-start(bf16[512,128]{1,0:T(8,128)(2,1)} %key.1) | copy-start | bytes 393220
  3.7 7.5 %copy-start.24 = (bf16[512,128]{1,0:T(8,128)(2,1)S(1)}, bf16[512,128]{1,0:T(8,128)(2,1)}, u32[]{:S(2)}) copy-start(bf16[512,128]{1,0:T(8,128)(2,1)} %value.1) | copy-start | bytes 393220
  3.7 7.5 %copy-start.25 = (bf16[128,512]{1,0:T(8,128)(2,1)S(1)}, bf16[128,512]{1,0:T(8,128)(2,1)}, u32[]{:S(2)}) copy-start(bf16[128,512]{1,0:T(8,128)(2,1)} %out.1) | copy-start | bytes 393220
  3.7 55.8 %all-to-all-start = ((bf16[8,2,128,512]{3,2,1,0:T(8,128)(2,1)}), bf16[8,2,128,512]{3,2,1,0:T(8,128)(2,1)}, u32[]{:S(2)}, u32[]{:S(2)}) async-start(bf16[8,2,128,512]{3,2,1,0:T(8,128)(2,1)} %pack_cotangent.1), calls=%async_computation | async-start | bytes 4194304 | tf_op jit(solution)/shard_map/all_to_all | solution.py:913
  11.2 16.2 %copy-start.6 = (bf16[2048,128]{1,0:T(8,128)(2,1)}, bf16[2048,128]{1,0:T(8,128)(2,1)S(1)}, u32[]{:S(2)}) copy-start(bf16[2048,128]{1,0:T(8,128)(2,1)S(1)} %pack_weights.1.refs_4_.refs_7_.refs_2_) | copy-start | bytes 1572868
  11.3 13.4 %collective-permute-start.1 = (bf16[2048,128]{1,0:T(8,128)(2,1)S(1)}, bf16[2048,128]{1,0:T(8,128)(2,1)S(1)}, u32[]{:S(2)}, u32[]{:S(2)}) collective-permute-start(bf16[2048,128]{1,0:T(8,128)(2,1)S(1)} %pack_weights.1.refs_4_.refs_7_.refs_2_), channel_id=1, source_target_pairs={{0,2},{1,3},{2,0},{3,1},{4,6},{5,7},{6,4},{7,5},{8,10},{9,11},{10,... | collective-permute-start | bytes 1572872 | tf_op jit(solution)/shard_map/ppermute | solution.py:909
  12.8 12.6 %collective-permute-start = (bf16[2048,128]{1,0:T(8,128)(2,1)S(1)}, bf16[2048,128]{1,0:T(8,128)(2,1)S(1)}, u32[]{:S(2)}, u32[]{:S(2)}) collective-permute-start(bf16[2048,128]{1,0:T(8,128)(2,1)S(1)} %pack_weights.1.refs_4_.refs_7_.refs_2_), channel_id=1, source_target_pairs={{0,1},{1,0},{2,3},{3,2},{4,5},{5,4},{6,7},{7,6},{8,9},{9,8},{10,11... | collective-permute-start | bytes 1572872 | tf_op jit(solution)/shard_map/ppermute | solution.py:909
  24.7 2.7 copy-start.44
  24.7 1.9 collective-permute-start.2
  25.4 2.0 copy-start.45
  59.5 29.7 %all-to-all-start.4 = ((bf16[8,128,512]{2,1,0:T(8,128)(2,1)}), bf16[8,128,512]{2,1,0:T(8,128)(2,1)S(1)}, u32[]{:S(2)}, u32[]{:S(2)}) async-start(bf16[8,128,512]{2,1,0:T(8,128)(2,1)} %bitcast.33), calls=%async_computation.4 | async-start | bytes 2097152 | tf_op jit(solution)/shard_map/all_to_all | solution.py:913
  84.9 8.0 %copy-start.47 = (bf16[512,8]{0,1:T(8,128)(2,1)S(1)}, bf16[512,8]{0,1:T(8,128)(2,1)}, u32[]{:S(2)}) copy-start(bf16[512,8]{0,1:T(8,128)(2,1)} %param.21) | copy-start | bytes 24580
  89.2 7.8 %copy-start.1 = (bf16[8,128,512]{2,1,0:T(8,128)(2,1)}, bf16[8,128,512]{2,1,0:T(8,128)(2,1)S(1)}, u32[]{:S(2)}) copy-start(bf16[8,128,512]{2,1,0:T(8,128)(2,1)S(1)} %all-to-all-done.4) | copy-start | bytes 3145732
  89.2 29.6 %all-to-all-start.1 = ((bf16[8,128,512]{2,1,0:T(8,128)(2,1)}), bf16[8,128,512]{2,1,0:T(8,128)(2,1)S(1)}, u32[]{:S(2)}, u32[]{:S(2)}) async-start(bf16[8,128,512]{2,1,0:T(8,128)(2,1)} %bitcast.34), calls=%async_computation.1 | async-start | bytes 2097152 | tf_op jit(solution)/shard_map/all_to_all | solution.py:913
  118.8 18.3 %all-to-all-start.5 = ((bf16[8,64,512]{2,1,0:T(8,128)(2,1)}), bf16[8,64,512]{2,1,0:T(8,128)(2,1)S(1)}, u32[]{:S(2)}, u32[]{:S(2)}) async-start(bf16[8,64,512]{2,1,0:T(8,128)(2,1)} %get-tuple-element.94), calls=%async_computation.5 | async-start | bytes 1048576 | tf_op jit(solution)/shard_map/all_to_all | solution.py:913
  122.5 18.3 %copy-start.33 = (f32[1,2048]{1,0:T(1,128)S(1)}, f32[1,2048]{1,0:T(1,128)}, u32[]{:S(2)}) copy-start(f32[1,2048]{1,0:T(1,128)} %b_expand.3) | copy-start | bytes 24580
  122.5 18.3 %copy-start.34 = (f32[1,512]{1,0:T(1,128)S(1)}, f32[1,512]{1,0:T(1,128)}, u32[]{:S(2)}) copy-start(f32[1,512]{1,0:T(1,128)} %b_reduce.3) | copy-start | bytes 6148
  137.1 12.1 %copy-start.13 = (bf16[8,64,512]{2,1,0:T(8,128)(2,1)}, bf16[8,64,512]{2,1,0:T(8,128)(2,1)S(1)}, u32[]{:S(2)}) copy-start(bf16[8,64,512]{2,1,0:T(8,128)(2,1)S(1)} %all-to-all-done.5) | copy-start | bytes 1572868
  137.1 18.3 %all-to-all-start.2 = ((bf16[8,64,512]{2,1,0:T(8,128)(2,1)}), bf16[8,64,512]{2,1,0:T(8,128)(2,1)S(1)}, u32[]{:S(2)}, u32[]{:S(2)}) async-start(bf16[8,64,512]{2,1,0:T(8,128)(2,1)} %get-tuple-element.89), calls=%async_computation.2 | async-start | bytes 1048576 | tf_op jit(solution)/shard_map/all_to_all | solution.py:913
  140.8 1.6 copy-start.27
  142.4 1.6 copy-start.29
  150.2 1.1 copy-start.37
  155.5 12.0 %copy-start.15 = (bf16[8,64,512]{2,1,0:T(8,128)(2,1)}, bf16[8,64,512]{2,1,0:T(8,128)(2,1)S(1)}, u32[]{:S(2)}) copy-start(bf16[8,64,512]{2,1,0:T(8,128)(2,1)S(1)} %all-to-all-done.2) | copy-start | bytes 1572868
  155.5 18.3 %all-to-all-start.6 = ((bf16[8,64,512]{2,1,0:T(8,128)(2,1)}), bf16[8,64,512]{2,1,0:T(8,128)(2,1)S(1)}, u32[]{:S(2)}, u32[]{:S(2)}) async-start(bf16[8,64,512]{2,1,0:T(8,128)(2,1)} %bitcast.12), calls=%async_computation.6 | async-start | bytes 1048576 | tf_op jit(solution)/shard_map/all_to_all | solution.py:913
  159.1 1.6 copy-start.28
  160.7 1.6 copy-start.30
  173.8 4.4 %copy-start.17 = (bf16[8,64,512]{2,1,0:T(8,128)(2,1)}, bf16[8,64,512]{2,1,0:T(8,128)(2,1)S(1)}, u32[]{:S(2)}) copy-start(bf16[8,64,512]{2,1,0:T(8,128)(2,1)S(1)} %all-to-all-done.6.answers) | copy-start | bytes 1572868
  173.8 19.7 %all-to-all-start.3 = ((bf16[8,64,512]{2,1,0:T(8,128)(2,1)}), bf16[8,64,512]{2,1,0:T(8,128)(2,1)}, u32[]{:S(2)}, u32[]{:S(2)}) async-start(bf16[8,64,512]{2,1,0:T(8,128)(2,1)} %bitcast.8), calls=%async_computation.3 | async-start | bytes 1048576 | tf_op jit(solution)/shard_map/all_to_all | solution.py:913
  178.1 1.2 copy-start.2
  179.4 1.0 copy-start.18
  180.4 1.0 copy-start.32
  181.5 5.5 %copy-start.14 = (bf16[8,64,512]{2,1,0:T(8,128)(2,1)S(1)}, bf16[8,64,512]{2,1,0:T(8,128)(2,1)}, u32[]{:S(2)}) copy-start(bf16[8,64,512]{2,1,0:T(8,128)(2,1)} %copy-done.13) | copy-start | bytes 1572868
  181.5 5.5 %copy-start.16 = (bf16[8,64,512]{2,1,0:T(8,128)(2,1)S(1)}, bf16[8,64,512]{2,1,0:T(8,128)(2,1)}, u32[]{:S(2)}) copy-start(bf16[8,64,512]{2,1,0:T(8,128)(2,1)} %copy-done.15) | copy-start | bytes 1572868
  181.5 5.5 %copy-start.26 = (s32[2]{0:T(128)S(1)}, s32[2]{0:T(128)}, u32[]{:S(2)}) copy-start(s32[2]{0:T(128)} %pad_add_fusion.refs_0_.place) | copy-start | bytes 28
  181.5 5.5 %copy-start.36 = (bf16[256,2048]{1,0:T(8,128)(2,1)S(1)}, bf16[256,2048]{1,0:T(8,128)(2,1)}, u32[]{:S(2)}) copy-start(bf16[256,2048]{1,0:T(8,128)(2,1)} %copy-done.35) | copy-start | bytes 3145732
  181.5 5.5 %copy-start.38 = (bf16[256,2048]{1,0:T(8,128)(2,1)S(1)}, bf16[256,2048]{1,0:T(8,128)(2,1)}, u32[]{:S(2)}) copy-start(bf16[256,2048]{1,0:T(8,128)(2,1)} %copy-done.37) | copy-start | bytes 3145732
  181.5 5.5 %copy-start.40 = (bf16[256,2048]{1,0:T(8,128)(2,1)S(1)}, bf16[256,2048]{1,0:T(8,128)(2,1)}, u32[]{:S(2)}) copy-start(bf16[256,2048]{1,0:T(8,128)(2,1)} %copy-done.39) | copy-start | bytes 3145732
  181.5 5.5 %copy-start.42 = (bf16[256,2048]{1,0:T(8,128)(2,1)S(1)}, bf16[256,2048]{1,0:T(8,128)(2,1)}, u32[]{:S(2)}) copy-start(bf16[256,2048]{1,0:T(8,128)(2,1)} %copy-done.41) | copy-start | bytes 3145732
  192.1 1.4 copy-start.3
  193.5 11.6 %collective-permute-start.3 = (bf16[2048,512]{1,0:T(8,128)(2,1)}, bf16[2048,512]{1,0:T(8,128)(2,1)}, u32[]{:S(2)}, u32[]{:S(2)}) collective-permute-start(bf16[2048,512]{1,0:T(8,128)(2,1)} %get-tuple-element.116), channel_id=1, source_target_pairs={{0,1},{1,0},{2,3},{3,2},{4,5},{5,4},{6,7},{7,6},{8,9},{9,8},{10,11... | collective-permute-start | bytes 6291464 | tf_op jit(solution)/shard_map/ppermute | solution.py:909
  193.5 32.5 %all-to-all-start.7 = ((bf16[8,128,512]{2,1,0:T(8,128)(2,1)}), bf16[8,128,512]{2,1,0:T(8,128)(2,1)}, u32[]{:S(2)}, u32[]{:S(2)}) async-start(bf16[8,128,512]{2,1,0:T(8,128)(2,1)} %bitcast.26), calls=%async_computation.7 | async-start | bytes 2097152 | tf_op jit(solution)/shard_map/all_to_all | solution.py:913
  199.5 1.0 copy-start.12
  200.5 4.6 %copy-start.4 = (bf16[2048,512]{1,0:T(8,128)(2,1)S(1)}, bf16[2048,512]{1,0:T(8,128)(2,1)}, u32[]{:S(2)}) copy-start(bf16[2048,512]{1,0:T(8,128)(2,1)} %copy-done.3) | copy-start | bytes 6291460
  205.0 4.7 %copy-start = (bf16[8,2,128,512]{3,2,1,0:T(8,128)(2,1)}, bf16[8,2,128,512]{3,2,1,0:T(8,128)(2,1)S(1)}, u32[]{:S(2)}) copy-start(bf16[8,2,128,512]{3,2,1,0:T(8,128)(2,1)S(1)} %get-tuple-element.105) | copy-start | bytes 6291460
  205.1 4.7 %copy-start.8 = (bf16[1024,512]{1,0:T(8,128)(2,1)}, bf16[1024,512]{1,0:T(8,128)(2,1)S(1)}, u32[]{:S(2)}) copy-start(bf16[1024,512]{1,0:T(8,128)(2,1)S(1)} %get-tuple-element.107) | copy-start | bytes 3145732
  209.8 51.6 %collective-permute-start.4 = (bf16[2048,512]{1,0:T(8,128)(2,1)}, bf16[2048,512]{1,0:T(8,128)(2,1)}, u32[]{:S(2)}, u32[]{:S(2)}) collective-permute-start(bf16[2048,512]{1,0:T(8,128)(2,1)} %add_convert_fusion.own), channel_id=1, source_target_pairs={{0,2},{1,3},{2,0},{3,1},{4,6},{5,7},{6,4},{7,5},{8,10},{9,11},{10,... | collective-permute-start | bytes 6291464 | tf_op jit(solution)/shard_map/ppermute | solution.py:909
  226.0 29.6 %all-to-all-start.9 = ((bf16[8,128,512]{2,1,0:T(8,128)(2,1)}), bf16[8,128,512]{2,1,0:T(8,128)(2,1)S(1)}, u32[]{:S(2)}, u32[]{:S(2)}) async-start(bf16[8,128,512]{2,1,0:T(8,128)(2,1)} %bitcast.27), calls=%async_computation.9 | async-start | bytes 2097152 | tf_op jit(solution)/shard_map/all_to_all | solution.py:913
  256.6 55.5 %all-to-all-start.8 = ((bf16[8,2,128,512]{3,2,1,0:T(8,128)(2,1)}), bf16[8,2,128,512]{3,2,1,0:T(8,128)(2,1)}, u32[]{:S(2)}, u32[]{:S(2)}) async-start(bf16[8,2,128,512]{3,2,1,0:T(8,128)(2,1)} %copy-done), calls=%async_computation.8 | async-start | bytes 4194304 | tf_op jit(solution)/shard_map/all_to_all | solution.py:913
  275.5 2.2 collective-permute-start.5
  275.5 36.5 %collective-permute-start.11 = (bf16[2048,512]{1,0:T(8,128)(2,1)}, bf16[2048,512]{1,0:T(8,128)(2,1)}, u32[]{:S(2)}, u32[]{:S(2)}) collective-permute-start(bf16[2048,512]{1,0:T(8,128)(2,1)} %add_convert_fusion.own), channel_id=1, source_target_pairs={{0,1},{1,0},{2,3},{3,2},{4,5},{5,4},{6,7},{7,6},{8,9},{9,8},{10,11... | collective-permute-start | bytes 6291464 | tf_op jit(solution)/shard_map/ppermute | solution.py:909
  276.0 36.1 %collective-permute-start.12 = (bf16[2048,512]{1,0:T(8,128)(2,1)}, bf16[2048,512]{1,0:T(8,128)(2,1)}, u32[]{:S(2)}, u32[]{:S(2)}) collective-permute-start(bf16[2048,512]{1,0:T(8,128)(2,1)} %collective-permute-done.4.own_across), channel_id=1, source_target_pairs={{0,1},{1,0},{2,3},{3,2},{4,5},{5,4},{6,7},{7,6},{8,9},{9,8},{10,11... | collective-permute-start | bytes 6291464 | tf_op jit(solution)/shard_map/ppermute | solution.py:909
  278.8 14.6 %collective-permute-start.6 = (bf16[2048,128]{1,0:T(8,128)(2,1)S(1)}, bf16[2048,128]{1,0:T(8,128)(2,1)S(1)}, u32[]{:S(2)}, u32[]{:S(2)}) collective-permute-start(bf16[2048,128]{1,0:T(8,128)(2,1)S(1)} %add_convert_fusion.1), channel_id=1, source_target_pairs={{0,2},{1,3},{2,0},{3,1},{4,6},{5,7},{6,4},{7,5},{8,10},{9,11},{10,... | collective-permute-start | bytes 1572872 | tf_op jit(solution)/shard_map/ppermute | solution.py:909
  280.4 14.3 %copy-start.48 = (f32[1,512]{1,0:T(1,128)S(1)}, f32[1,512]{1,0:T(1,128)}, u32[]{:S(2)}) copy-start(f32[1,512]{1,0:T(1,128)} %get-tuple-element.104) | copy-start | bytes 6148
  280.4 14.3 %copy-start.49 = (f32[1,512]{1,0:T(1,128)S(1)}, f32[1,512]{1,0:T(1,128)}, u32[]{:S(2)}) copy-start(f32[1,512]{1,0:T(1,128)} %get-tuple-element.139) | copy-start | bytes 6148
  293.4 15.5 %collective-permute-start.7 = (bf16[2048,128]{1,0:T(8,128)(2,1)}, bf16[2048,128]{1,0:T(8,128)(2,1)S(1)}, u32[]{:S(2)}, u32[]{:S(2)}) collective-permute-start(bf16[2048,128]{1,0:T(8,128)(2,1)} %get-tuple-element.135), channel_id=1, source_target_pairs={{0,1},{1,0},{2,3},{3,2},{4,5},{5,4},{6,7},{7,6},{8,9},{9,8},{10,11... | collective-permute-start | bytes 1572872 | tf_op jit(solution)/shard_map/ppermute | solution.py:909
  306.8 5.3 %collective-permute-start.10 = (f32[21,512]{1,0:T(8,128)S(1)}, f32[21,512]{1,0:T(8,128)S(1)}, u32[]{:S(2)}, u32[]{:S(2)}) collective-permute-start(f32[21,512]{1,0:T(8,128)S(1)} %concatenate.3.refs_0_), channel_id=1, source_target_pairs={{0,3},{1,2},{2,1},{3,0},{4,7},{5,6},{6,5},{7,4},{8,11},{9,10},{10,... | collective-permute-start | bytes 129032 | tf_op jit(solution)/shard_map/ppermute | solution.py:909
  307.8 4.3 %collective-permute-start.9 = (f32[21,512]{1,0:T(8,128)S(1)}, f32[21,512]{1,0:T(8,128)S(1)}, u32[]{:S(2)}, u32[]{:S(2)}) collective-permute-start(f32[21,512]{1,0:T(8,128)S(1)} %concatenate.3.refs_0_), channel_id=1, source_target_pairs={{0,2},{1,3},{2,0},{3,1},{4,6},{5,7},{6,4},{7,5},{8,10},{9,11},{10,... | collective-permute-start | bytes 129032 | tf_op jit(solution)/shard_map/ppermute | solution.py:909
  309.8 2.3 collective-permute-start.8
  309.8 1.0 copy-start.19
  311.8 25.9 %copy-start.9 = (bf16[1024,512]{1,0:T(8,128)(2,1)S(1)}, bf16[1024,512]{1,0:T(8,128)(2,1)}, u32[]{:S(2)}) copy-start(bf16[1024,512]{1,0:T(8,128)(2,1)} %get-tuple-element.84.refs_1_.refs_0_) | copy-start | bytes 3145732
  311.9 25.9 %copy-start.10 = (bf16[1024,512]{1,0:T(8,128)(2,1)S(1)}, bf16[1024,512]{1,0:T(8,128)(2,1)}, u32[]{:S(2)}) copy-start(bf16[1024,512]{1,0:T(8,128)(2,1)} %get-tuple-element.85.refs_1_) | copy-start | bytes 3145732
  334.1 21.1 %all-to-all-start.11 = ((bf16[8,320,128]{2,1,0:T(8,128)(2,1)}), bf16[8,320,128]{2,1,0:T(8,128)(2,1)S(1)}, u32[]{:S(2)}, u32[]{:S(2)}) async-start(bf16[8,320,128]{2,1,0:T(8,128)(2,1)} %get-tuple-element.143), calls=%async_computation.11 | async-start | bytes 1310720 | tf_op jit(solution)/shard_map/all_to_all | solution.py:913
  (10 other events, 9.2 us)
